TPU v7x, 512 devices: a whole 4x8x8 slice. The times are simulated.
512 devices in a mesh: rep: 8 (over x, core), tp: 32 (over z_hi, y), fsdp: 2 (over z_lo).
Axes of the slice: x: 4, y: 8, z: 8 (z_hi: 4, z_lo: 2; z = z_hi * 2 + z_lo), core: 2. Of those that a mesh axis runs over, the one named last changes fastest.
Arguments:
- tokens: bfloat16 [4, 1024, 2048], P(None, ('rep', 'fsdp'), 'tp'), may hold values from -6 to 6
- norm_gain: bfloat16 [2048], replicated, may hold values from 0.5 to 2
- router: bfloat16 [2048, 8], replicated, may hold values from -0.125 to 0.125
- routes: int32 [4, 1024, 2], P(None, ('rep', 'fsdp')), may hold values from 0 to 7, all different within a row; in each aligned block of 64 rows (0 to 63, 64 to 127, ..., all dimensions but the last counted through in order) at most 32 rows name the same one
- expert_weights: bfloat16 [32, 2048, 768], P('tp'), may hold values from -0.125 to 0.125
- codes: bfloat16 [32, 2048, 768], P('tp', ('rep', 'fsdp')), may hold values from -6 to 6
- scales: bfloat16 [32, 2048, 48], P('tp', ('rep', 'fsdp')), may hold values from 0.0019989014 to 0.019897461
- owner_map: int32 [2048], replicated, may hold values from 0 to 2047, each once
Outputs:
- mixed: bfloat16 [4, 1024, 2048], P(None, ('rep', 'fsdp'), 'tp')
Inputs may be any that keep to these rules, and one draw needn't show every extreme that they name: `owner_map`: each number appears once. `routes`: a row names 2 different experts; within one step's 64 rows of one rollout group (aligned blocks of 64 rows), no expert is named by more than 32 rows, a bound that some block reaches.
All inputs are finite; a program needn't handle non-finite values.
Results may differ from a plain program's by a relative error of at most 0.02.
Values may be sent and summed in bfloat16 or wider, within the bound.
A program may use at most 64 MiB of HBM per device.

v0:
```python
import jax
import jax.numpy as jnp
from jax import lax
from jax.sharding import PartitionSpec as P

SPLIT = 4


def dequantize(values, factors):
    count, width = values.shape
    blocks = factors.shape[1]
    column = jnp.arange(width, dtype=jnp.int32) // (width // blocks)
    spread = (column[None, :] == jnp.arange(blocks, dtype=jnp.int32)[:, None]).astype(jnp.float32)
    stretched = jnp.dot(factors.astype(jnp.float32), spread, precision=lax.Precision.HIGHEST)
    return values.astype(jnp.float32) * stretched


def expert_piece(normed, share, fresh):
    inner = fresh.shape[1] // 3
    both = jnp.einsum(
        "rd,df->rf", normed, fresh[:, : 2 * inner], preferred_element_type=jnp.float32
    )
    hidden = (jax.nn.silu(both[:, :inner]) * both[:, inner:] * share[:, None]).astype(jnp.bfloat16)
    part = jnp.einsum(
        "rf,df->rd", hidden, fresh[:, 2 * inner :], preferred_element_type=jnp.float32
    )
    return lax.optimization_barrier(part.astype(jnp.bfloat16)).astype(jnp.float32)


def body(tokens, norm_gain, router, routes, expert_weights, codes, scales, owner_map):
    whole = lax.all_gather(tokens, "tp", axis=2, tiled=True)
    inverse = jnp.argsort(owner_map)
    pieces = expert_weights[0]
    got_codes, got_scales = (
        lax.all_gather(codes, ("rep", "fsdp"), axis=1, tiled=True),
        lax.all_gather(scales, ("rep", "fsdp"), axis=1, tiled=True),
    )
    delta = jnp.take(dequantize(got_codes[0], got_scales[0]), inverse, axis=0)
    fresh = (pieces.astype(jnp.float32) + delta).astype(jnp.bfloat16)
    inputs = whole.astype(jnp.float32)
    meansq = jnp.mean(inputs * inputs, axis=-1, keepdims=True)
    normed = (inputs * lax.rsqrt(meansq + 1e-06) * norm_gain.astype(jnp.float32)).astype(
        jnp.bfloat16
    )
    logits = jnp.einsum("srd,de->sre", normed, router, preferred_element_type=jnp.float32)
    chosen = jax.nn.sigmoid(jnp.take_along_axis(logits, routes, axis=-1))
    gates = chosen / jnp.sum(chosen, axis=-1, keepdims=True)
    expert = lax.axis_index("tp") // SPLIT
    share = jnp.sum(jnp.where(routes == expert, gates, 0.0), axis=-1)
    steps_count, row_count, width = whole.shape
    results = []
    for step in range(steps_count):
        terms = expert_piece(normed[step], share[step], fresh)
        results.append(
            lax.psum_scatter(
                terms.astype(jnp.bfloat16), "tp", scatter_dimension=1, tiled=True
            ).astype(jnp.float32)
        )
    summed = jnp.stack(results, axis=0)
    return (tokens.astype(jnp.float32) + summed).astype(jnp.bfloat16)


def solution(mesh):
    placed = (
        P(None, ("rep", "fsdp"), "tp"),
        P(),
        P(),
        P(None, ("rep", "fsdp"), None),
        P("tp", None, None),
        P("tp", ("rep", "fsdp"), None),
        P("tp", ("rep", "fsdp"), None),
        P(),
    )
    return jax.shard_map(
        body, mesh=mesh, in_specs=placed, out_specs=P(None, ("rep", "fsdp"), "tp"), check_vma=False
    )
```

profile of v0, /device:TPU:2, one launch (start us, length us, event | category | flops | bytes accessed | tf_op | source)
XLA Modules:
  0.0 1101.9 jit_solution(8219041020011671614)
XLA Ops:
  6.5 1.6 copy.45
  8.2 1.8 copy.47
  10.7 0.7 bitcast_or_fusion
  11.7 5.7 sort.17
  17.4 29.6 %all_gather.11 = bf16[1,2048,48]{1,2,0:T(8,128)(2,1)S(1)} all-gather(bf16[1,128,48]{1,2,0:T(8,128)(2,1)} %param.14), channel_id=1, replica_groups=mesh['rep'=8,'tp'=32,'fsdp'=2] {'rep','fsdp'}, dimensions={1}, use_global_device_ids=true | all-gather | bytes 208896 | tf_op jit(solution)/shard_map/all_gather | solution.py:36
  47.0 55.7 %all-gather.3.cloned.1.call-done = bf16[4,64,2048]{1,0,2:T(4,128)(2,1)} async-done(((bf16[4,64,64]{1,0,2:T(4,128)(2,1)}), bf16[4,64,2048]{1,0,2:T(4,128)(2,1)}) %all-gather.3.cloned.1.call-update) | async-done | bytes 1048592 | tf_op jit(solution)/shard_map/all_gather | solution.py:31
  102.7 2.9 copy.46
  106.8 3.5 gather_fusion.1
  110.6 43.2 %all-gather.5.cloned.1.call-done = bf16[1,2048,768]{1,2,0:T(8,128)(2,1)} async-done(((bf16[1,128,768]{1,2,0:T(8,128)(2,1)}), bf16[1,2048,768]{1,2,0:T(8,128)(2,1)}) %all-gather.5.cloned.1.call-update) | async-done | bytes 3145744 | tf_op jit(solution)/shard_map/all_gather | solution.py:35
  153.8 5.6 convert_multiply_fusion
  159.4 6.5 copy.48
  165.9 13.4 %gather_fusion = f32[2048,768]{1,0:T(8,128)} fusion(f32[2048,768]{1,0:T(8,128)} %copy.48, s32[2048]{0:T(1024)S(1)} %fusion.40), kind=kCustom, calls=%fused_computation | custom fusion | bytes 12591104 | tf_op jit(solution)/shard_map/jit(_take)/gather | solution.py:38
  179.3 4.2 fusion
  184.0 1.2 copy-done.1
  185.6 1.0 copy.61
  186.7 2.1 fusion.6
  188.8 1.7 convolution_convert_fusion.1
  190.5 1.0 copy.59
  191.6 2.1 fusion.8
  193.6 1.7 convolution_convert_fusion.2
  195.3 1.0 copy.57
  196.4 2.1 fusion.10
  198.4 1.7 convolution_convert_fusion.3
  200.1 1.0 copy.55
  201.1 211.6 %reduce-scatter.19.cloned.1.call-done = bf16[64,64]{1,0:T(8,128)(2,1)} async-done(((bf16[2048,64]{1,0:T(8,128)(2,1)}), bf16[64,64]{1,0:T(8,128)(2,1)}) %reduce-scatter.19.cloned.1.call-update) | async-done | bytes 8208
  412.7 0.8 copy.62
  413.5 225.7 %reduce-scatter.17.cloned.1.call-done = bf16[64,64]{1,0:T(8,128)(2,1)} async-done(((bf16[2048,64]{1,0:T(8,128)(2,1)}), bf16[64,64]{1,0:T(8,128)(2,1)}) %reduce-scatter.17.cloned.1.call-update) | async-done | bytes 8208
  639.3 0.8 copy.60
  640.1 225.2 %reduce-scatter.15.cloned.1.call-done = bf16[64,64]{1,0:T(8,128)(2,1)} async-done(((bf16[2048,64]{1,0:T(8,128)(2,1)}), bf16[64,64]{1,0:T(8,128)(2,1)}) %reduce-scatter.15.cloned.1.call-update) | async-done | bytes 8208
  865.3 0.8 copy.58
  866.1 227.5 %reduce-scatter.13.cloned.1.call-done = bf16[64,64]{1,0:T(8,128)(2,1)} async-done(((bf16[2048,64]{1,0:T(8,128)(2,1)}), bf16[64,64]{1,0:T(8,128)(2,1)}) %reduce-scatter.13.cloned.1.call-update) | async-done | bytes 8208
  1093.5 0.8 copy.56
  (38 shorter events, 4.3 us)
Async XLA Ops:
  6.5 99.8 %copy-start = (bf16[2048,8]{0,1:T(8,128)(2,1)S(1)}, bf16[2048,8]{0,1:T(8,128)(2,1)}, u32[]{:S(2)}) copy-start(bf16[2048,8]{0,1:T(8,128)(2,1)} %param.10) | copy-start | bytes 98308
  6.5 96.2 %all-gather.3.cloned.1.call-start = ((), (), s32[]{:S(2)}) async-start(), calls=%async_computation.4 | async-start | bytes 2162688 | tf_op jit(solution)/shard_map/all_gather | solution.py:31
  8.1 145.7 %all-gather.5.cloned.1.call-start = ((), (), s32[]{:S(2)}) async-start(), calls=%async_computation.5 | async-start | bytes 3342336 | tf_op jit(solution)/shard_map/all_gather | solution.py:35
  10.0 402.8 %reduce-scatter.19.cloned.1.call-start = ((), (), s32[]{:S(2)}) async-start(), calls=%async_computation.9 | async-start | bytes 540672
  106.8 3.7 copy-start.3
  183.5 1.7 copy-start.1
  186.7 452.6 %reduce-scatter.17.cloned.1.call-start = ((), (), s32[]{:S(2)}) async-start(), calls=%async_computation.8 | async-start | bytes 540672
  191.5 673.8 %reduce-scatter.15.cloned.1.call-start = ((), (), s32[]{:S(2)}) async-start(), calls=%async_computation.7 | async-start | bytes 540672
  196.3 898.1 %copy-start.2 = (bf16[4,64,64]{2,1,0:T(8,128)(2,1)S(1)}, bf16[4,64,64]{2,1,0:T(8,128)(2,1)}, u32[]{:S(2)}) copy-start(bf16[4,64,64]{2,1,0:T(8,128)(2,1)} %param.8) | copy-start | bytes 98308
  196.3 897.2 %reduce-scatter.13.cloned.1.call-start = ((), (), s32[]{:S(2)}) async-start(), calls=%async_computation.6 | async-start | bytes 540672
Sparse Core Ops, SparseCore 0:
  10.5 92.1 all-gather.2
  104.8 48.9 all-gather.4
  186.8 225.9 reduce-scatter.18
  417.7 221.5 reduce-scatter.16
  643.6 221.6 reduce-scatter.14
  870.2 223.2 reduce-scatter.12
where the time goes:
time: 1100 us
  waiting for transfers between devices  989 us (90%)
  local copies, waits for them, and re-layouts  38.5 us (4%)
  blocking collectives  29.6 us (3%)
  matrix products  18.2 us (2%)
  between operations  13.7 us (1%)
  other arithmetic  12.7 us (1%)
    unnamed x10, waiting for transfers between devices  890 us
    all_gather x1, waiting for transfers between devices, body(): whole = lax.all_gather(tokens, 'tp', axis=2, tiled=True)  55.7 us
    all_gather x1, waiting for transfers between devices, body(): lax.all_gather(codes, ('rep', 'fsdp'), axis=1, tiled=True)  43.2 us
    all_gather x1, blocking collectives, body(): lax.all_gather(scales, ('rep', 'fsdp'), axis=1, tiled=True)  29.6 us
  transfers between devices with their start and end apart: 6, of which 6 were waited for; matrix products, arithmetic and copies ran while one was open for 3% of the time, Pallas kernels for 0%

commit v1 on v0

v1 whole, which is shorter than its diff:
```python
import jax
import jax.numpy as jnp
from jax import lax
from jax.experimental import pallas as pl
from jax.experimental.pallas import tpu as pltpu
from jax.sharding import PartitionSpec as P

MESH = pl.DeviceIdType.MESH
BF = jnp.bfloat16
F32 = jnp.float32
NX, NZ, NY, NT, NE, CAP = 4, 4, 8, 32, 8, 32
D, F = 2048, 256


def mm(a, b, ca=1, cb=0):
    return lax.dot_general(a, b, (((ca,), (cb,)), ((), ())), preferred_element_type=F32)


def iota(shape, dim):
    return lax.broadcasted_iota(jnp.int32, shape, dim)


def kernel(
    tok_ref, gain_ref, router_ref, routes_ref, w_hbm, codes_ref, scales_ref, om_ref, out_ref,
    w, gu, dn, perm, cmat, ctmat, msg, xr, xn, xp, outm, outr, wsem, ss, rs, ts, tr, os, orr,
):
    rep, tp, zl = lax.axis_index("rep"), lax.axis_index("tp"), lax.axis_index("fsdp")
    x, c = rep // 2, rep % 2
    zh, y = tp // NY, tp % NY
    e0 = tp // 4
    xd, xu, x2 = (x + NX - 1) % NX, (x + 1) % NX, (x + 2) % NX

    def peer(kind):
        if kind == "core":
            return {"rep": x * 2 + (1 - c)}
        if kind == "z":
            return {"fsdp": 1 - zl}
        return {"rep": (xu if kind == "up" else xd) * 2 + c}

    def tdev(k):
        return ((zh + k // NY) % NZ) * NY + (y + k % NY) % NY

    bar = pltpu.get_barrier_semaphore()
    for kind in ("core", "z", "up", "down"):
        pl.semaphore_signal(bar, inc=1, device_id=peer(kind), device_id_type=MESH)

    @pl.loop(1, NT)
    def _(k):
        pl.semaphore_signal(bar, inc=1, device_id={"tp": tdev(k)}, device_id_type=MESH)

    wcopy = pltpu.make_async_copy(w_hbm.at[0], w, wsem)
    wcopy.start()

    own = rep * 2 + zl
    spread = (iota((48, 768), 1) // 16 == iota((48, 768), 0)).astype(BF)
    delta = (codes_ref[0].astype(F32) * mm(scales_ref[0], spread)).astype(BF)
    gu[own] = delta[:, :512]
    dn[own] = delta[:, 512:]

    rt = routes_ref[...].reshape(256, 2)
    lane = iota((256, 128), 1)
    hit = ((rt[:, 0:1] == lane) | (rt[:, 1:2] == lane)).astype(F32)
    hitb = hit.astype(BF)
    ra, rb = iota((256, 256), 0), iota((256, 256), 1)
    before = ((rb < ra) & (ra // 64 == rb // 64)).astype(BF)
    pos = mm(before, hitb)
    expand = (iota((128, 256), 0) == iota((128, 256), 1) // CAP).astype(BF)
    hitx = mm(hitb, expand)
    posx = mm(pos.astype(BF), expand)
    ct = jnp.where(posx == (rb % CAP).astype(F32), hitx, 0.0)
    ctmat[...] = ct.astype(BF)
    cm = ct.T.astype(BF)
    cmat[...] = cm
    tok = tok_ref[...].reshape(256, 64)
    tok2 = jnp.concatenate([tok, tok], axis=1)
    want = iota((256, 128), 0) // 64
    half = lane // 64
    for j in range(2):
        placed = jnp.where(want == 2 * j + half, tok2.astype(F32), 0.0).astype(BF)
        msg[:, j] = mm(cm, placed).astype(BF).reshape(NE, CAP, 128)

    pl.semaphore_wait(bar, 35)

    bufs = (gu, dn)
    sent = []

    def shard(xx, cc, zz):
        return (xx * 2 + cc) * 2 + zz

    def send(part, o, h, kind):
        ref = bufs[part].at[o] if h is None else bufs[part].at[o, pl.ds(64 * h, 64)]
        cp = pltpu.make_async_remote_copy(
            src_ref=ref, dst_ref=ref, send_sem=ss.at[len(sent)],
            recv_sem=rs.at[part, o, 0 if h is None else h],
            device_id=peer(kind), device_id_type=MESH,
        )
        cp.start()
        sent.append(cp)

    def recv(part, o, h):
        ref = bufs[part].at[o] if h is None else bufs[part].at[o, pl.ds(64 * h, 64)]
        pltpu.make_async_remote_copy(
            src_ref=ref, dst_ref=ref, send_sem=ss.at[0],
            recv_sem=rs.at[part, o, 0 if h is None else h],
            device_id=peer("core"), device_id_type=MESH,
        ).wait_recv()

    def first(part):
        send(part, own, 0, "z")
        send(part, own, 0, "up")
        send(part, own, 1, "down")
        send(part, own, 1, "z")
        send(part, own, 1, "up")
        send(part, own, 0, "down")
        send(part, own, None, "core")

    def second(part):
        o = shard(x, c, 1 - zl)
        recv(part, o, 0)
        send(part, o, 0, "up")
        recv(part, o, 1)
        send(part, o, 1, "down")
        send(part, o, 1, "up")
        send(part, o, 0, "down")
        send(part, o, None, "core")

    def third(part, zz):
        lo, hi = shard(xd, c, zz), shard(xu, c, zz)
        recv(part, lo, 0)
        send(part, lo, 0, "up")
        recv(part, hi, 1)
        send(part, hi, 1, "down")
        recv(part, lo, 1)
        send(part, lo, None, "core")
        recv(part, hi, 0)
        send(part, hi, None, "core")

    def fourth(part, zz):
        o = shard(x2, c, zz)
        recv(part, o, 0)
        recv(part, o, 1)
        send(part, o, None, "core")

    def fifth(part):
        for xx in range(NX):
            for zz in range(2):
                recv(part, shard(xx, 1 - c, zz), None)

    first(0)

    def tcopy(k):
        t = tdev(k)
        return pltpu.make_async_remote_copy(
            src_ref=msg.at[t // 4], dst_ref=xr.at[tp], send_sem=ts.at[k], recv_sem=tr.at[tp],
            device_id={"tp": t}, device_id_type=MESH,
        )

    def twait(k):
        t = tdev(k)
        return pltpu.make_async_remote_copy(
            src_ref=msg.at[0], dst_ref=xr.at[t], send_sem=ts.at[k], recv_sem=tr.at[t],
            device_id={"tp": t}, device_id_type=MESH,
        )

    @pl.loop(1, NT)
    def _(k):
        tcopy(k).start()

    xr[tp] = msg[e0]

    def build(lo, hi):
        @pl.loop(lo, hi)
        def _(i):
            base = pl.multiple_of(i * 128, 128)
            perm[pl.ds(base, 128), :] = jnp.where(
                iota((128, D), 0) + base == om_ref[...], 1.0, 0.0
            ).astype(BF)

    build(0, 8)
    second(0)
    build(8, 16)
    third(0, zl)
    first(1)
    third(0, 1 - zl)

    @pl.loop(1, NT)
    def _(k):
        twait(k).wait_recv()

    low = iota((64, 128), 1) < 64
    for u in range(NT // 2):
        a = xr[2 * u].reshape(64, 128).astype(F32)
        b = xr[2 * u + 1].reshape(64, 128).astype(F32)
        xn[:64, 128 * u : 128 * u + 128] = jnp.where(low, a, pltpu.roll(b, 64, 1)).astype(BF)
        xn[64:, 128 * u : 128 * u + 128] = jnp.where(low, pltpu.roll(a, 64, 1), b).astype(BF)
    rows = xn[...].astype(F32)
    scale = lax.rsqrt(jnp.mean(rows * rows, axis=-1, keepdims=True) + 1e-06)
    xn[...] = (rows * scale * gain_ref[...].astype(F32)).astype(BF)

    second(1)
    fourth(0, zl)
    fourth(0, 1 - zl)

    logits = mm(xn[...], router_ref[...])
    mine = cmat[pl.ds(pl.multiple_of(e0 * CAP, CAP), CAP), :].astype(F32)
    four = jnp.concatenate([mine, mine, mine, mine], axis=0)
    rowid = iota((128, 256), 0)
    step = (rowid // 32 % 2) * 2 + rowid // 64
    chosen = mm(jnp.where(iota((128, 256), 1) // 64 == step, four, 0.0).astype(BF), hitb)[:, :NE]
    sig = jax.nn.sigmoid(logits) * chosen
    total = jnp.sum(sig, axis=-1, keepdims=True)
    this = jnp.sum(jnp.where(iota((128, NE), 1) == e0, sig, 0.0), axis=-1, keepdims=True)
    used = jnp.sum(chosen, axis=-1, keepdims=True) > 0.5
    share = jnp.where(used, this / jnp.where(used, total, 1.0), 0.0)

    @pl.loop(0, 8)
    def _(i):
        at = pl.ds(pl.multiple_of(i * 256, 256), 256)
        xp[:, at] = mm(xn[...], perm[:, at]).astype(BF)

    third(1, zl)
    third(1, 1 - zl)
    wcopy.wait()
    both = mm(xn[...], w[:, : 2 * F])
    fifth(0)
    both = both + mm(xp[...], gu[...].reshape(D, 2 * F))
    hidden = (jax.nn.silu(both[:, :F]) * both[:, F:] * share).astype(BF)
    fourth(1, zl)
    fourth(1, 1 - zl)
    fifth(1)
    xp[...] = mm(hidden, dn[...].reshape(D, F), 1, 1).astype(BF)

    def odest(k):
        return ((tp // 4 + k // 4) % NE) * 4 + (tp % 4 + k % 4) % 4

    def ocopy(k):
        t = odest(k)
        return pltpu.make_async_remote_copy(
            src_ref=outm.at[t], dst_ref=outr.at[tp % 4, tp // 4], send_sem=os.at[k],
            recv_sem=orr.at[tp], device_id={"tp": t}, device_id_type=MESH,
        )

    def owait(k):
        t = odest(k)
        return pltpu.make_async_remote_copy(
            src_ref=outm.at[t], dst_ref=outr.at[t % 4, t // 4], send_sem=os.at[k],
            recv_sem=orr.at[t], device_id={"tp": t}, device_id_type=MESH,
        )

    @pl.loop(0, 8)
    def _(i):
        g = (tp // 4 + i) % NE
        at = pl.ds(pl.multiple_of(g * 256, 256), 256)
        part = mm(hidden, w[at, 2 * F :], 1, 1) + mm(xp[...], perm[at, :], 1, 1)
        for u in range(2):
            even, odd = part[:64, 128 * u : 128 * u + 128], part[64:, 128 * u : 128 * u + 128]
            outm[g * 4 + 2 * u] = jnp.where(low, even, pltpu.roll(odd, 64, 1)).astype(BF).reshape(2, CAP, 128)
            outm[g * 4 + 2 * u + 1] = jnp.where(low, pltpu.roll(even, 64, 1), odd).astype(BF).reshape(2, CAP, 128)

        @pl.when(i > 0)
        def _():
            ocopy(4 * i).start()

        for q in range(1, 4):
            ocopy(4 * i + q).start()

    outr[tp % 4, tp // 4] = outm[tp]

    for cp in sent:
        cp.wait_send()

    @pl.loop(1, NT)
    def _(k):
        tcopy(k).wait_send()
        owait(k).wait_recv()

    for j in range(2):
        acc = jnp.zeros((128, 128), F32)
        for q in range(4):
            acc = acc + mm(ctmat[128 * j : 128 * j + 128, :], outr[q, :, j].reshape(256, 128))
        for a in range(2):
            s = 2 * j + a
            out_ref[s] = (
                tok_ref[s].astype(F32) + acc[64 * a : 64 * a + 64, 64 * a : 64 * a + 64]
            ).astype(BF)

    @pl.loop(1, NT)
    def _(k):
        ocopy(k).wait_send()


def body(tokens, norm_gain, router, routes, expert_weights, codes, scales, owner_map):
    vm = pl.BlockSpec(memory_space=pltpu.VMEM)
    dma = pltpu.SemaphoreType.DMA
    return pl.pallas_call(
        kernel,
        out_shape=jax.ShapeDtypeStruct(tokens.shape, BF),
        in_specs=[vm, vm, vm, vm, pl.BlockSpec(memory_space=pl.ANY), vm, vm, vm],
        out_specs=vm,
        scratch_shapes=[
            pltpu.VMEM((D, 3 * F), BF),
            pltpu.VMEM((16, 128, 2 * F), BF),
            pltpu.VMEM((16, 128, F), BF),
            pltpu.VMEM((D, D), BF),
            pltpu.VMEM((256, 256), BF),
            pltpu.VMEM((256, 256), BF),
            pltpu.VMEM((NE, 2, CAP, 128), BF),
            pltpu.VMEM((NT, 2, CAP, 128), BF),
            pltpu.VMEM((128, D), BF),
            pltpu.VMEM((128, D), BF),
            pltpu.VMEM((NT, 2, CAP, 128), BF),
            pltpu.VMEM((4, NE, 2, CAP, 128), BF),
            dma, dma((48,)), dma((2, 16, 2)),
            dma((NT,)), dma((NT,)), dma((NT,)), dma((NT,)),
        ],
        compiler_params=pltpu.CompilerParams(
            collective_id=0, has_side_effects=True, vmem_limit_bytes=48 << 20
        ),
        cost_estimate=pl.CostEstimate(flops=4 * 10**9, bytes_accessed=8 << 20, transcendentals=0),
    )(
        tokens, norm_gain.reshape(1, D), router, routes, expert_weights, codes, scales,
        owner_map.reshape(1, D),
    )


def solution(mesh):
    placed = (
        P(None, ("rep", "fsdp"), "tp"),
        P(),
        P(),
        P(None, ("rep", "fsdp"), None),
        P("tp", None, None),
        P("tp", ("rep", "fsdp"), None),
        P("tp", ("rep", "fsdp"), None),
        P(),
    )
    return jax.shard_map(
        body, mesh=mesh, in_specs=placed, out_specs=P(None, ("rep", "fsdp"), "tp"), check_vma=False
    )
```

time: 1100 us -> 77.3 us (0.07)
  the two profiles are of different devices: /device:TPU:2 before, /device:TPU:73 now
where the time goes in v1:
time: 77.3 us; the launch traced here: 76.8 us
  Pallas kernels  68.5 us (89%)
  local copies, waits for them, and re-layouts  8.32 us (11%)
    pallas_call x1, Pallas kernels, body(): pl.pallas_call(kernel, out_shape=jax.ShapeDtypeStruct(tokens.shape, BF),...  68.5 us
    unnamed x12, local copies, waits for them, and re-layouts  7.63 us

profile of v1, /device:TPU:73, one launch (start us, length us, event | category | flops | bytes accessed | tf_op | source)
XLA Modules:
  0.0 76.8 jit_solution(7345733380628339292)
XLA Ops:
  0.0 0.7 reshape.6.gain_ref
  0.7 0.8 %copy.11.scales_ref = bf16[1,128,48]{2,1,0:T(8,128)(2,1)S(1)} copy(bf16[1,128,48]{1,2,0:T(8,128)(2,1)} %param.14) | data formatting | bytes 24576 | tf_op args[6]
  1.5 0.8 %copy.10.routes_ref = s32[4,64,2]{2,1,0:T(8,128)S(1)} copy(s32[4,64,2]{1,2,0:T(2,128)} %param.11) | data formatting | bytes 4096 | tf_op args[3]
  2.3 1.0 %copy.9.router_ref = bf16[2048,8]{1,0:T(8,128)(2,1)S(1)} copy(bf16[2048,8]{0,1:T(8,128)(2,1)} %param.10) | data formatting | bytes 65536 | tf_op args[2]
  3.4 0.0 copy-start
  3.4 1.9 %copy-done = bf16[1,2048,768]{2,1,0:T(8,128)(2,1)S(1)} copy-done((bf16[1,2048,768]{2,1,0:T(8,128)(2,1)S(1)}, bf16[1,2048,768]{2,1,0:T(8,128)(2,1)}, u32[]{:S(2)}) %copy-start) | copy-done | bytes 3145752
  5.3 0.0 copy-start.1
  5.3 0.9 %copy-done.1 = bf16[1,128,768]{2,1,0:T(8,128)(2,1)S(1)} copy-done((bf16[1,128,768]{2,1,0:T(8,128)(2,1)S(1)}, bf16[1,128,768]{2,1,0:T(8,128)(2,1)}, u32[]{:S(2)}) %copy-start.1) | copy-done | bytes 196632
  6.2 0.0 copy-start.2
  6.2 0.8 %copy-done.2 = bf16[4,64,64]{2,1,0:T(8,128)(2,1)S(1)} copy-done((bf16[4,64,64]{2,1,0:T(8,128)(2,1)S(1)}, bf16[4,64,64]{2,1,0:T(8,128)(2,1)}, u32[]{:S(2)}) %copy-start.2) | copy-done | bytes 32792
  7.0 0.0 copy-start.3
  7.0 0.7 copy-done.3
  7.7 68.5 %shard_map.82 = bf16[4,64,64]{2,1,0:T(8,128)(2,1)S(1)} custom-call(bf16[4,64,64]{2,1,0:T(8,128)(2,1)S(1)} %copy-done.2, bf16[1,2048]{1,0:T(2,128)(2,1)S(1)} %reshape.6.gain_ref, bf16[2048,8]{1,0:T(8,128)(2,1)S(1)} %copy.9.router_ref, s32[4,64,2]{2,1,0:T(8,128)S(1)} %copy.10.routes_ref, bf16[1,2048,768]{2,1,0:T(8,128)(2,1)S(1)} %copy-done, ...), custom_call_target="tpu_custom_call" | custom-call | flops 4000000000 | bytes 8388608 | tf_op jit(solution)/shard_map/pallas_call | solution.py:295
  76.2 0.6 copy.13
Async XLA Ops:
  3.4 1.9 %copy-start = (bf16[1,2048,768]{2,1,0:T(8,128)(2,1)S(1)}, bf16[1,2048,768]{2,1,0:T(8,128)(2,1)}, u32[]{:S(2)}) copy-start(bf16[1,2048,768]{2,1,0:T(8,128)(2,1)} %w_hbm.1) | copy-start | bytes 9437188
  5.3 0.9 %copy-start.1 = (bf16[1,128,768]{2,1,0:T(8,128)(2,1)S(1)}, bf16[1,128,768]{2,1,0:T(8,128)(2,1)}, u32[]{:S(2)}) copy-start(bf16[1,128,768]{2,1,0:T(8,128)(2,1)} %codes_ref.1) | copy-start | bytes 589828
  6.2 0.8 %copy-start.2 = (bf16[4,64,64]{2,1,0:T(8,128)(2,1)S(1)}, bf16[4,64,64]{2,1,0:T(8,128)(2,1)}, u32[]{:S(2)}) copy-start(bf16[4,64,64]{2,1,0:T(8,128)(2,1)} %tok_ref.1) | copy-start | bytes 98308
  7.0 0.7 copy-start.3

commit v2 on v1

--- a/solution.py
+++ b/solution.py
@@ -21,8 +21,8 @@
 
 
 def kernel(
-    tok_ref, gain_ref, router_ref, routes_ref, w_hbm, codes_ref, scales_ref, om_ref, out_ref,
-    w, gu, dn, perm, cmat, ctmat, msg, xr, xn, xp, outm, outr, wsem, ss, rs, ts, tr, os, orr,
+    tok_hbm, gain_hbm, router_hbm, routes_hbm, w_hbm, codes_hbm, scales_hbm, om_hbm, out_ref,
+    tok_ref, gain_ref, router_ref, routes_ref, codes_ref, scales_ref, om_ref, grow, w, gu, dn, perm, cmat, ctmat, msg, xr, xn, xp, outm, outr, wsem, ss, rs, ts, tr, os, orr,
 ):
     rep, tp, zl = lax.axis_index("rep"), lax.axis_index("tp"), lax.axis_index("fsdp")
     x, c = rep // 2, rep % 2
@@ -48,18 +48,34 @@
     def _(k):
         pl.semaphore_signal(bar, inc=1, device_id={"tp": tdev(k)}, device_id_type=MESH)
 
-    wcopy = pltpu.make_async_copy(w_hbm.at[0], w, wsem)
-    wcopy.start()
+    pairs = (
+        (codes_hbm.at[0], codes_ref), (scales_hbm.at[0], scales_ref), (routes_hbm, routes_ref),
+        (tok_hbm, tok_ref), (om_hbm, om_ref), (router_hbm, router_ref), (gain_hbm, gain_ref),
+        (w_hbm.at[0], w),
+    )
+    loads = [pltpu.make_async_copy(a, b, wsem.at[i]) for i, (a, b) in enumerate(pairs)]
+    for cp in loads:
+        cp.start()
+    loads[0].wait()
+    loads[1].wait()
 
     own = rep * 2 + zl
     spread = (iota((48, 768), 1) // 16 == iota((48, 768), 0)).astype(BF)
-    delta = (codes_ref[0].astype(F32) * mm(scales_ref[0], spread)).astype(BF)
+    delta = (codes_ref[...].astype(F32) * mm(scales_ref[...], spread, 0, 0)).astype(BF)
     gu[own] = delta[:, :512]
     dn[own] = delta[:, 512:]
 
-    rt = routes_ref[...].reshape(256, 2)
+    loads[2].wait()
+    loads[3].wait()
     lane = iota((256, 128), 1)
-    hit = ((rt[:, 0:1] == lane) | (rt[:, 1:2] == lane)).astype(F32)
+    name = iota((128, 64), 0)
+    hit = jnp.concatenate(
+        [
+            ((routes_ref[s, 0:1, :] == name) | (routes_ref[s, 1:2, :] == name)).astype(F32).T
+            for s in range(4)
+        ],
+        axis=0,
+    )
     hitb = hit.astype(BF)
     ra, rb = iota((256, 256), 0), iota((256, 256), 1)
     before = ((rb < ra) & (ra // 64 == rb // 64)).astype(BF)
@@ -147,6 +163,8 @@
                 recv(part, shard(xx, 1 - c, zz), None)
 
     first(0)
+    for cp in loads[4:7]:
+        cp.wait()
 
     def tcopy(k):
         t = tdev(k)
@@ -193,15 +211,17 @@
         b = xr[2 * u + 1].reshape(64, 128).astype(F32)
         xn[:64, 128 * u : 128 * u + 128] = jnp.where(low, a, pltpu.roll(b, 64, 1)).astype(BF)
         xn[64:, 128 * u : 128 * u + 128] = jnp.where(low, pltpu.roll(a, 64, 1), b).astype(BF)
+    for u in range(16):
+        grow[:, 128 * u : 128 * u + 128] = gain_ref[u : u + 1, :].astype(F32)
     rows = xn[...].astype(F32)
     scale = lax.rsqrt(jnp.mean(rows * rows, axis=-1, keepdims=True) + 1e-06)
-    xn[...] = (rows * scale * gain_ref[...].astype(F32)).astype(BF)
+    xn[...] = (rows * scale * grow[...]).astype(BF)
 
     second(1)
     fourth(0, zl)
     fourth(0, 1 - zl)
 
-    logits = mm(xn[...], router_ref[...])
+    logits = mm(xn[...], router_ref[...], 1, 1)
     mine = cmat[pl.ds(pl.multiple_of(e0 * CAP, CAP), CAP), :].astype(F32)
     four = jnp.concatenate([mine, mine, mine, mine], axis=0)
     rowid = iota((128, 256), 0)
@@ -220,7 +240,7 @@
 
     third(1, zl)
     third(1, 1 - zl)
-    wcopy.wait()
+    loads[7].wait()
     both = mm(xn[...], w[:, : 2 * F])
     fifth(0)
     both = both + mm(xp[...], gu[...].reshape(D, 2 * F))
@@ -295,9 +315,17 @@
     return pl.pallas_call(
         kernel,
         out_shape=jax.ShapeDtypeStruct(tokens.shape, BF),
-        in_specs=[vm, vm, vm, vm, pl.BlockSpec(memory_space=pl.ANY), vm, vm, vm],
+        in_specs=[pl.BlockSpec(memory_space=pltpu.HBM)] * 8,
         out_specs=vm,
         scratch_shapes=[
+            pltpu.VMEM((4, 64, 64), BF),
+            pltpu.VMEM((16, 128), BF),
+            pltpu.VMEM((NE, D), BF),
+            pltpu.VMEM((4, 2, 64), jnp.int32),
+            pltpu.VMEM((128, 3 * F), BF),
+            pltpu.VMEM((48, 128), BF),
+            pltpu.VMEM((1, D), jnp.int32),
+            pltpu.VMEM((1, D), F32),
             pltpu.VMEM((D, 3 * F), BF),
             pltpu.VMEM((16, 128, 2 * F), BF),
             pltpu.VMEM((16, 128, F), BF),
@@ -310,16 +338,16 @@
             pltpu.VMEM((128, D), BF),
             pltpu.VMEM((NT, 2, CAP, 128), BF),
             pltpu.VMEM((4, NE, 2, CAP, 128), BF),
-            dma, dma((48,)), dma((2, 16, 2)),
+            dma((8,)), dma((48,)), dma((2, 16, 2)),
             dma((NT,)), dma((NT,)), dma((NT,)), dma((NT,)),
         ],
         compiler_params=pltpu.CompilerParams(
-            collective_id=0, has_side_effects=True, vmem_limit_bytes=48 << 20
+            collective_id=0, has_side_effects=True, vmem_limit_bytes=60 << 20
         ),
         cost_estimate=pl.CostEstimate(flops=4 * 10**9, bytes_accessed=8 << 20, transcendentals=0),
     )(
-        tokens, norm_gain.reshape(1, D), router, routes, expert_weights, codes, scales,
-        owner_map.reshape(1, D),
+        tokens, norm_gain.reshape(16, 128), router.T, routes.transpose(0, 2, 1), expert_weights,
+        codes, scales.transpose(0, 2, 1), owner_map.reshape(1, D),
     )
 
 

time: 77.3 us -> 71.7 us (0.928)
  the two profiles are of different devices: /device:TPU:73 before, /device:TPU:1 now
where the time goes in v2:
time: 71.7 us; the launch traced here: 71.5 us
  Pallas kernels  70 us (98%)
  local copies, waits for them, and re-layouts  1.47 us (2%)
    pallas_call x1, Pallas kernels, body(): pl.pallas_call(kernel, out_shape=jax.ShapeDtypeStruct(tokens.shape, BF),...  70 us
    unnamed x1, local copies, waits for them, and re-layouts  1.47 us

profile of v2, /device:TPU:1, one launch (start us, length us, event | category | flops | bytes accessed | tf_op | source)
XLA Modules:
  0.0 71.5 jit_solution(15145763298796706465)
XLA Ops:
  0.0 70.0 %shard_map.82 = bf16[4,64,64]{2,1,0:T(8,128)(2,1)} custom-call(bf16[4,64,64]{2,1,0:T(8,128)(2,1)} %tok_hbm.1, bf16[16,128]{1,0:T(8,128)(2,1)} %bitcast.8, bf16[8,2048]{1,0:T(8,128)(2,1)} %bitcast.5, s32[4,2,64]{2,1,0:T(2,128)} %bitcast.9, bf16[1,2048,768]{2,1,0:T(8,128)(2,1)} %w_hbm.1, bf16[1,128,768]{2,1,0:T(8,128)(2,1)} %codes_hbm.1, ...), custom_call_target="tpu_custom_call" | custom-call | flops 4000000000 | bytes 8388608 | tf_op jit(solution)/shard_map/pallas_call | solution.py:315
  70.0 1.5 %copy.10 = bf16[4,64,64]{2,1,0:T(8,128)(2,1)} copy(bf16[4,64,64]{2,1,0:T(8,128)(2,1)} %shard_map.82) | data formatting | bytes 65536

commit v3 on v2

v3 whole, which is shorter than its diff:
```python
import jax
import jax.numpy as jnp
from jax import lax
from jax.experimental import pallas as pl
from jax.experimental.pallas import tpu as pltpu
from jax.sharding import PartitionSpec as P

MESH = pl.DeviceIdType.MESH
BF = jnp.bfloat16
F32 = jnp.float32
NX, NZ, NY, NE, CAP = 4, 4, 8, 8, 32
D, F = 2048, 256
ZB = D // NZ


def mm(a, b, ca=1, cb=0):
    return lax.dot_general(a, b, (((ca,), (cb,)), ((), ())), preferred_element_type=F32)


def iota(shape, dim):
    return lax.broadcasted_iota(jnp.int32, shape, dim)


def kernel(
    tok_hbm, gain_hbm, router_hbm, routes_hbm, w_hbm, codes_hbm, scales_hbm, om_hbm, out_ref,
    tok_ref, gain_ref, router_ref, routes_ref, codes_ref, scales_ref, om_ref, grow, omrow,
    w, gu, dn, perm, cmat, ctmat, msg, zm, xr, xg, xacc, xp, outm, outr, zs, zr,
    wsem, dsend, drecv, dcore, zsend, zrecv, ysend, yrecv, osend, orecv, psend, precv,
):
    rep, tp, zl = lax.axis_index("rep"), lax.axis_index("tp"), lax.axis_index("fsdp")
    x, c = rep // 2, rep % 2
    zh, y = tp // NY, tp % NY
    e0 = tp // 4
    x1, x2, x3 = (x + 1) % NX, (x + 2) % NX, (x + 3) % NX

    def peer(kind):
        if kind == "core":
            return {"rep": x * 2 + (1 - c)}
        if kind == "z":
            return {"fsdp": 1 - zl}
        return {"rep": (x1 if kind == "up" else x3) * 2 + c}

    def ydev(r):
        return {"tp": zh * NY + (y + r) % NY}

    def zdev(r):
        return {"tp": ((zh + r) % NZ) * NY + y}

    def remote(src, dst, ssem, rsem, dev):
        return pltpu.make_async_remote_copy(
            src_ref=src, dst_ref=dst, send_sem=ssem, recv_sem=rsem, device_id=dev,
            device_id_type=MESH,
        )

    bar = pltpu.get_barrier_semaphore()
    partners = [peer(k) for k in ("core", "z", "up", "down")]
    partners += [ydev(r) for r in range(1, NY)] + [zdev(r) for r in range(1, NZ)]
    for dev in partners:
        pl.semaphore_signal(bar, inc=1, device_id=dev, device_id_type=MESH)

    pairs = (
        (codes_hbm.at[0], codes_ref), (scales_hbm.at[0], scales_ref), (routes_hbm, routes_ref),
        (tok_hbm, tok_ref), (om_hbm, om_ref), (router_hbm, router_ref), (gain_hbm, gain_ref),
        (w_hbm.at[0], w),
    )
    loads = [pltpu.make_async_copy(a, b, wsem.at[i]) for i, (a, b) in enumerate(pairs)]
    for cp in loads:
        cp.start()

    loads[0].wait()
    loads[1].wait()

    def block(cc, xx, zz):
        return cc * 8 + xx * 2 + zz

    own = block(c, x, zl)
    spread = (iota((48, 768), 1) // 16 == iota((48, 768), 0)).astype(BF)
    delta = (codes_ref[...].astype(F32) * mm(scales_ref[...], spread, 0, 0)).astype(BF)
    gu[own] = delta[:, : 2 * F]
    dn[own] = delta[:, 2 * F :]

    loads[2].wait()
    loads[3].wait()
    lane = iota((256, 128), 1)
    name = iota((128, 64), 0)
    hit = jnp.concatenate(
        [
            ((routes_ref[s, 0:1, :] == name) | (routes_ref[s, 1:2, :] == name)).astype(F32).T
            for s in range(4)
        ],
        axis=0,
    )
    hitb = hit.astype(BF)
    ra, rb = iota((256, 256), 0), iota((256, 256), 1)
    before = ((rb < ra) & (ra // 64 == rb // 64)).astype(BF)
    pos = mm(before, hitb)
    expand = (iota((128, 256), 0) == iota((128, 256), 1) // CAP).astype(BF)
    hitx = mm(hitb, expand)
    posx = mm(pos.astype(BF), expand)
    ct = jnp.where(posx == (rb % CAP).astype(F32), hitx, 0.0)
    ctmat[...] = ct.astype(BF)
    cm = ct.T.astype(BF)
    cmat[...] = cm
    tok = tok_ref[...].reshape(256, 64)
    tok2 = jnp.concatenate([tok, tok], axis=1)
    want = iota((256, 128), 0) // 64
    half = lane // 64
    for j in range(2):
        placed = jnp.where(want == 2 * j + half, tok2.astype(F32), 0.0).astype(BF)
        msg[:, j] = mm(cm, placed).astype(BF).reshape(NE, CAP, 128)

    pl.semaphore_wait(bar, len(partners))

    bufs = (gu, dn)

    def send(part, o, h, kind):
        ref = bufs[part].at[o] if h is None else bufs[part].at[o, pl.ds(64 * h, 64)]
        sem = dcore.at[part] if kind == "core" else drecv.at[part, o, 0 if h is None else h]
        remote(ref, ref, dsend.at[part], sem, peer(kind)).start()

    def recv(part, o, h):
        ref = bufs[part].at[o] if h is None else bufs[part].at[o, pl.ds(64 * h, 64)]
        sem = drecv.at[part, o, 0 if h is None else h]
        remote(ref, ref, dsend.at[part], sem, peer("core")).wait_recv()

    def spread_x(part, o):
        send(part, o, 0, "up")
        send(part, o, 1, "down")
        send(part, o, 1, "up")
        send(part, o, 0, "down")

    def first(part):
        send(part, own, None, "z")
        spread_x(part, own)
        send(part, own, None, "core")

    def second(part):
        o = block(c, x, 1 - zl)
        recv(part, o, None)
        spread_x(part, o)
        send(part, o, None, "core")

    def third(part, zz):
        lo, hi = block(c, x3, zz), block(c, x1, zz)
        recv(part, lo, 0)
        send(part, lo, 0, "up")
        recv(part, hi, 1)
        send(part, hi, 1, "down")
        recv(part, lo, 1)
        send(part, lo, None, "core")
        recv(part, hi, 0)
        send(part, hi, None, "core")

    def fourth(part, zz):
        o = block(c, x2, zz)
        recv(part, o, 0)
        recv(part, o, 1)
        send(part, o, None, "core")

    def fifth(part):
        ref = bufs[part].at[pl.ds(8 * (1 - c), 8)]
        remote(ref, ref, dsend.at[part], dcore.at[part], peer("core")).wait_recv()

    def zcopy(r, src):
        return remote(msg.at[pl.ds(2 * ((zh + r) % NZ), 2)], zm.at[src], zsend.at[r], zrecv.at[src], zdev(r))

    def zget(r):
        src = (zh + r) % NZ
        zcopy(r, src).wait_recv()
        yput(src)

    def yput(src):
        for r in range(1, NY):
            to = (y + r) % NY
            remote(zm.at[src, to // 4], xr.at[src, y], ysend.at[src], yrecv.at[src], ydev(r)).start()
        pltpu.make_async_copy(zm.at[src, y // 4], xr.at[src, y], yrecv.at[src]).start()

    for r in (1, 3, 2):
        zcopy(r, zh).start()
    zm[zh] = msg[pl.ds(2 * zh, 2)]
    first(0)
    yput(zh)

    for cp in loads[4:7]:
        cp.wait()
    for cc in range(2):
        for xx in range(NX):
            for zz in range(2):
                s = (xx * 2 + cc) * 2 + zz
                b = block(cc, xx, zz)
                omrow[:, 128 * b : 128 * b + 128] = om_ref[:, 128 * s : 128 * s + 128]
    for u in range(16):
        grow[:, 128 * u : 128 * u + 128] = gain_ref[u : u + 1, :].astype(F32)

    def build(lo, hi):
        @pl.loop(lo, hi)
        def _(i):
            base = pl.multiple_of(i * 128, 128)
            perm[pl.ds(base, 128), :] = jnp.where(
                iota((128, D), 0) + base == omrow[...], 1.0, 0.0
            ).astype(BF)

    low = iota((64, 128), 1) < 64

    def quarter(r, carry):
        zz = (zh + r) % NZ
        remote(xr.at[zz], xr.at[zz], ysend.at[zz], yrecv.at[zz], ydev(1)).wait_recv()
        ssq, wacc, lacc = carry
        for u in range(NY // 2):
            a = xr[zz, 2 * u].reshape(64, 128).astype(F32)
            b = xr[zz, 2 * u + 1].reshape(64, 128).astype(F32)
            g = grow[:, pl.ds(pl.multiple_of(zz * ZB + 128 * u, 128), 128)]
            even = jnp.where(low, a, pltpu.roll(b, 64, 1))
            odd = jnp.where(low, pltpu.roll(a, 64, 1), b)
            ssq = ssq + jnp.concatenate([even * even, odd * odd], axis=0)
            xg[:64, 128 * u : 128 * u + 128] = (even * g).astype(BF)
            xg[64:, 128 * u : 128 * u + 128] = (odd * g).astype(BF)
        at = pl.ds(pl.multiple_of(zz * ZB, ZB), ZB)
        wacc = wacc + mm(xg[...], w[at, : 2 * F])
        lacc = lacc + mm(xg[...], router_ref[:, at], 1, 1)

        @pl.loop(0, 4)
        def _(i):
            cols = pl.ds(pl.multiple_of(i * 512, 512), 512)
            got = mm(xg[...], perm[at, cols])
            if r == 0:
                xacc[:, cols] = got
            else:
                xacc[:, cols] += got

        return ssq, wacc, lacc

    build(0, 8)
    zget(1)
    zget(3)
    second(0)
    zget(2)
    first(1)
    build(8, 16)
    third(0, zl)
    second(1)
    loads[7].wait()
    carry = (jnp.zeros((128, 128), F32), jnp.zeros((128, 2 * F), F32), jnp.zeros((128, NE), F32))
    carry = quarter(0, carry)
    third(0, 1 - zl)
    third(1, zl)
    carry = quarter(1, carry)
    fourth(0, zl)
    fourth(0, 1 - zl)
    third(1, 1 - zl)
    carry = quarter(3, carry)
    fourth(1, zl)
    ssq, wacc, lacc = quarter(2, carry)

    scale = lax.rsqrt(jnp.sum(ssq, axis=-1, keepdims=True) * (1.0 / D) + 1e-06)
    mine = cmat[pl.ds(pl.multiple_of(e0 * CAP, CAP), CAP), :].astype(F32)
    four = jnp.concatenate([mine, mine, mine, mine], axis=0)
    rowid = iota((128, 256), 0)
    step = (rowid // 32 % 2) * 2 + rowid // 64
    chosen = mm(jnp.where(iota((128, 256), 1) // 64 == step, four, 0.0).astype(BF), hitb)[:, :NE]
    sig = jax.nn.sigmoid(lacc * scale) * chosen
    total = jnp.sum(sig, axis=-1, keepdims=True)
    this = jnp.sum(jnp.where(iota((128, NE), 1) == e0, sig, 0.0), axis=-1, keepdims=True)
    used = jnp.sum(chosen, axis=-1, keepdims=True) > 0.5
    share = jnp.where(used, this / jnp.where(used, total, 1.0), 0.0)
    xp[...] = xacc[...].astype(BF)

    def halfmm(cc):
        at = pl.ds(pl.multiple_of(cc * (D // 2), D // 2), D // 2)
        return mm(xp[:, at], gu[pl.ds(8 * cc, 8)].reshape(D // 2, 2 * F))

    both = wacc + halfmm(c)
    fifth(0)
    both = (both + halfmm(1 - c)) * scale
    hidden = (jax.nn.silu(both[:, :F]) * both[:, F:] * share).astype(BF)
    fourth(1, 1 - zl)
    fifth(1)
    xp[...] = mm(hidden, dn[...].reshape(D, F), 1, 1).astype(BF)

    for r in (1, 2, 3, 0):
        zz = (zh + r) % NZ
        at = pl.ds(pl.multiple_of(zz * ZB, ZB), ZB)
        part = mm(hidden, w[at, 2 * F :], 1, 1) + mm(xp[...], perm[at, :], 1, 1)
        for u in range(NY // 2):
            even, odd = part[:64, 128 * u : 128 * u + 128], part[64:, 128 * u : 128 * u + 128]
            outm[zz, 2 * u] = jnp.where(low, even, pltpu.roll(odd, 64, 1)).astype(BF).reshape(2, CAP, 128)
            outm[zz, 2 * u + 1] = jnp.where(low, pltpu.roll(even, 64, 1), odd).astype(BF).reshape(2, CAP, 128)
        for k in range(1, NY):
            remote(outm.at[zz, (y + k) % NY], outr.at[zz, y], osend.at[r], orecv.at[zz], ydev(k)).start()
        pltpu.make_async_copy(outm.at[zz, y], outr.at[zz, y], orecv.at[zz]).start()

    def sums(r):
        zz = (zh + r) % NZ
        remote(outr.at[zz], outr.at[zz], osend.at[r], orecv.at[zz], ydev(1)).wait_recv()
        got = outr[zz].astype(F32)
        return jnp.stack([jnp.sum(got[:4], axis=0), jnp.sum(got[4:], axis=0)]).astype(BF)

    def pcopy(r, src):
        return remote(zs.at[r], zr.at[src], psend.at[r], precv.at[src], zdev(r))

    for r in (1, 2, 3):
        zs[r] = sums(r)
        pcopy(r, zh).start()
    zr[zh] = sums(0)
    for r in (1, 2, 3):
        pcopy(r, (zh + r) % NZ).wait_recv()

    for j in range(2):
        acc = mm(ctmat[128 * j : 128 * j + 128, :], zr[:, :, j].reshape(256, 128))
        for a in range(2):
            s = 2 * j + a
            out_ref[s] = (
                tok_ref[s].astype(F32) + acc[64 * a : 64 * a + 64, 64 * a : 64 * a + 64]
            ).astype(BF)

    for r in (1, 2, 3):
        zcopy(r, zh).wait_send()
        pcopy(r, zh).wait_send()
    for part in range(2):
        ref = bufs[part].at[pl.ds(0, 15)]
        remote(ref, ref, dsend.at[part], dcore.at[part], peer("core")).wait_send()
    for r in range(NZ):
        ref = xr.at[r, pl.ds(0, NY - 1)]
        remote(ref, ref, ysend.at[r], yrecv.at[r], ydev(1)).wait_send()
        remote(ref, ref, osend.at[r], orecv.at[r], ydev(1)).wait_send()


def body(tokens, norm_gain, router, routes, expert_weights, codes, scales, owner_map):
    dma = pltpu.SemaphoreType.DMA
    vm = pltpu.VMEM
    return pl.pallas_call(
        kernel,
        out_shape=jax.ShapeDtypeStruct(tokens.shape, BF),
        in_specs=[pl.BlockSpec(memory_space=pltpu.HBM)] * 8,
        out_specs=pl.BlockSpec(memory_space=pltpu.VMEM),
        scratch_shapes=[
            vm((4, 64, 64), BF),
            vm((16, 128), BF),
            vm((NE, D), BF),
            vm((4, 2, 64), jnp.int32),
            vm((128, 3 * F), BF),
            vm((48, 128), BF),
            vm((1, D), jnp.int32),
            vm((1, D), F32),
            vm((1, D), jnp.int32),
            vm((D, 3 * F), BF),
            vm((16, 128, 2 * F), BF),
            vm((16, 128, F), BF),
            vm((D, D), BF),
            vm((256, 256), BF),
            vm((256, 256), BF),
            vm((NE, 2, CAP, 128), BF),
            vm((NZ, 2, 2, CAP, 128), BF),
            vm((NZ, NY, 2, CAP, 128), BF),
            vm((128, ZB), BF),
            vm((128, D), F32),
            vm((128, D), BF),
            vm((NZ, NY, 2, CAP, 128), BF),
            vm((NZ, NY, 2, CAP, 128), BF),
            vm((NZ, 2, 2, CAP, 128), BF),
            vm((NZ, 2, 2, CAP, 128), BF),
            dma((8,)), dma((2,)), dma((2, 16, 2)), dma((2,)),
            dma((NZ,)), dma((NZ,)), dma((NZ,)), dma((NZ,)),
            dma((NZ,)), dma((NZ,)), dma((NZ,)), dma((NZ,)),
        ],
        compiler_params=pltpu.CompilerParams(
            collective_id=0, has_side_effects=True, vmem_limit_bytes=60 << 20
        ),
        cost_estimate=pl.CostEstimate(flops=4 * 10**9, bytes_accessed=8 << 20, transcendentals=0),
    )(
        tokens, norm_gain.reshape(16, 128), router.T, routes.transpose(0, 2, 1), expert_weights,
        codes, scales.transpose(0, 2, 1), owner_map.reshape(1, D),
    )


def solution(mesh):
    placed = (
        P(None, ("rep", "fsdp"), "tp"),
        P(),
        P(),
        P(None, ("rep", "fsdp"), None),
        P("tp", None, None),
        P("tp", ("rep", "fsdp"), None),
        P("tp", ("rep", "fsdp"), None),
        P(),
    )
    return jax.shard_map(
        body, mesh=mesh, in_specs=placed, out_specs=P(None, ("rep", "fsdp"), "tp"), check_vma=False
    )
```

time: 71.7 us -> 57.2 us (0.80)
  Pallas kernels: 70 us -> 55.6 us
    pallas_call x1, Pallas kernels: 70 us -> 55.6 us  [body(): pl.pallas_call(kernel, out_shape=jax.ShapeDtypeStruct(tokens.shape, BF),...]
where the time goes in v3:
time: 57.2 us; the launch traced here: 57 us
  Pallas kernels  55.6 us (97%)
  local copies, waits for them, and re-layouts  1.47 us (3%)
    pallas_call x1, Pallas kernels, body(): pl.pallas_call(kernel, out_shape=jax.ShapeDtypeStruct(tokens.shape, BF),...  55.6 us
    unnamed x1, local copies, waits for them, and re-layouts  1.47 us

profile of v3, /device:TPU:1, one launch (start us, length us, event | category | flops | bytes accessed | tf_op | source)
XLA Modules:
  0.0 57.0 jit_solution(13263630716978560997)
XLA Ops:
  0.0 55.6 %shard_map.82 = bf16[4,64,64]{2,1,0:T(8,128)(2,1)} custom-call(bf16[4,64,64]{2,1,0:T(8,128)(2,1)} %tok_hbm.1, bf16[16,128]{1,0:T(8,128)(2,1)} %bitcast.8, bf16[8,2048]{1,0:T(8,128)(2,1)} %bitcast.5, s32[4,2,64]{2,1,0:T(2,128)} %bitcast.9, bf16[1,2048,768]{2,1,0:T(8,128)(2,1)} %w_hbm.1, bf16[1,128,768]{2,1,0:T(8,128)(2,1)} %codes_hbm.1, ...), custom_call_target="tpu_custom_call" | custom-call | flops 4000000000 | bytes 8388608 | tf_op jit(solution)/shard_map/pallas_call | solution.py:331
  55.6 1.5 %copy.10 = bf16[4,64,64]{2,1,0:T(8,128)(2,1)} copy(bf16[4,64,64]{2,1,0:T(8,128)(2,1)} %shard_map.82) | data formatting | bytes 65536

commit v4 on v3

--- a/solution.py
+++ b/solution.py
@@ -11,6 +11,7 @@
 NX, NZ, NY, NE, CAP = 4, 4, 8, 8, 32
 D, F = 2048, 256
 ZB = D // NZ
+FAR = (4, 3, 5, 2, 6, 1, 7)
 
 
 def mm(a, b, ca=1, cb=0):
@@ -24,7 +25,7 @@
 def kernel(
     tok_hbm, gain_hbm, router_hbm, routes_hbm, w_hbm, codes_hbm, scales_hbm, om_hbm, out_ref,
     tok_ref, gain_ref, router_ref, routes_ref, codes_ref, scales_ref, om_ref, grow, omrow,
-    w, gu, dn, perm, cmat, ctmat, msg, zm, xr, xg, xacc, xp, outm, outr, zs, zr,
+    w, gu, dn, perm, ptw, hy, cmat, ctmat, msg, zm, xr, xg, xacc, xp, outm, outr, zs, zr,
     wsem, dsend, drecv, dcore, zsend, zrecv, ysend, yrecv, osend, orecv, psend, precv,
 ):
     rep, tp, zl = lax.axis_index("rep"), lax.axis_index("tp"), lax.axis_index("fsdp")
@@ -52,14 +53,8 @@
             device_id_type=MESH,
         )
 
-    bar = pltpu.get_barrier_semaphore()
-    partners = [peer(k) for k in ("core", "z", "up", "down")]
-    partners += [ydev(r) for r in range(1, NY)] + [zdev(r) for r in range(1, NZ)]
-    for dev in partners:
-        pl.semaphore_signal(bar, inc=1, device_id=dev, device_id_type=MESH)
-
     pairs = (
-        (codes_hbm.at[0], codes_ref), (scales_hbm.at[0], scales_ref), (routes_hbm, routes_ref),
+        (scales_hbm.at[0], scales_ref), (codes_hbm.at[0], codes_ref), (routes_hbm, routes_ref),
         (tok_hbm, tok_ref), (om_hbm, om_ref), (router_hbm, router_ref), (gain_hbm, gain_ref),
         (w_hbm.at[0], w),
     )
@@ -67,17 +62,91 @@
     for cp in loads:
         cp.start()
 
+    bar = pltpu.get_barrier_semaphore()
+    partners = [peer(k) for k in ("core", "z", "up", "down")]
+    partners += [ydev(r) for r in range(1, NY)] + [zdev(r) for r in range(1, NZ)]
+    for dev in partners:
+        pl.semaphore_signal(bar, inc=1, device_id=dev, device_id_type=MESH)
+
     loads[0].wait()
     loads[1].wait()
 
     def block(cc, xx, zz):
         return cc * 8 + xx * 2 + zz
 
+    def slots(b, n=1):
+        return pl.ds(pl.multiple_of(b * 128, 128), n * 128)
+
     own = block(c, x, zl)
     spread = (iota((48, 768), 1) // 16 == iota((48, 768), 0)).astype(BF)
-    delta = (codes_ref[...].astype(F32) * mm(scales_ref[...], spread, 0, 0)).astype(BF)
-    gu[own] = delta[:, : 2 * F]
-    dn[own] = delta[:, 2 * F :]
+    delta = codes_ref[...].astype(F32) * mm(scales_ref[...], spread, 0, 0)
+    gu[own] = delta[:, : 2 * F].astype(BF)
+    dn[:, slots(own)] = delta[:, 2 * F :].T.astype(BF)
+
+    pl.semaphore_wait(bar, len(partners))
+
+    def shard(part, o, h):
+        if part == 0:
+            return gu.at[o] if h is None else gu.at[o, pl.ds(64 * h, 64)]
+        return dn.at[:, slots(o)] if h is None else dn.at[pl.ds(128 * h, 128), slots(o)]
+
+    def send(part, o, h, kind):
+        ref = shard(part, o, h)
+        sem = dcore.at[part] if kind == "core" else drecv.at[part, o, h]
+        remote(ref, ref, dsend.at[part], sem, peer(kind)).start()
+
+    def recv(part, o, h):
+        ref = shard(part, o, h)
+        remote(ref, ref, dsend.at[part], drecv.at[part, o, h], peer("core")).wait_recv()
+
+    def core(part, o):
+        send(part, o, None, "core")
+
+    def first():
+        for part in range(2):
+            send(part, own, 0, "z")
+            send(part, own, 1, "z")
+            send(part, own, 0, "up")
+            send(part, own, 1, "down")
+            send(part, own, 1, "up")
+            send(part, own, 0, "down")
+        core(0, own)
+        core(1, own)
+
+    def pair(part):
+        o = block(c, x, 1 - zl)
+        recv(part, o, 0)
+        send(part, o, 0, "up")
+        send(part, o, 0, "down")
+        recv(part, o, 1)
+        send(part, o, 1, "down")
+        send(part, o, 1, "up")
+
+    def onward(part, zz):
+        lo, hi = block(c, x3, zz), block(c, x1, zz)
+        recv(part, lo, 0)
+        send(part, lo, 0, "up")
+        recv(part, hi, 1)
+        send(part, hi, 1, "down")
+
+    def near(part, zz):
+        lo, hi = block(c, x3, zz), block(c, x1, zz)
+        recv(part, lo, 1)
+        core(part, lo)
+        recv(part, hi, 0)
+        core(part, hi)
+
+    def far(part, zz):
+        o = block(c, x2, zz)
+        recv(part, o, 0)
+        recv(part, o, 1)
+        core(part, o)
+
+    def other(part):
+        ref = gu.at[pl.ds(8 * (1 - c), 8)] if part == 0 else dn.at[:, slots(8 * (1 - c), 8)]
+        remote(ref, ref, dsend.at[part], dcore.at[part], peer("core")).wait_recv()
+
+    first()
 
     loads[2].wait()
     loads[3].wait()
@@ -109,58 +178,6 @@
         placed = jnp.where(want == 2 * j + half, tok2.astype(F32), 0.0).astype(BF)
         msg[:, j] = mm(cm, placed).astype(BF).reshape(NE, CAP, 128)
 
-    pl.semaphore_wait(bar, len(partners))
-
-    bufs = (gu, dn)
-
-    def send(part, o, h, kind):
-        ref = bufs[part].at[o] if h is None else bufs[part].at[o, pl.ds(64 * h, 64)]
-        sem = dcore.at[part] if kind == "core" else drecv.at[part, o, 0 if h is None else h]
-        remote(ref, ref, dsend.at[part], sem, peer(kind)).start()
-
-    def recv(part, o, h):
-        ref = bufs[part].at[o] if h is None else bufs[part].at[o, pl.ds(64 * h, 64)]
-        sem = drecv.at[part, o, 0 if h is None else h]
-        remote(ref, ref, dsend.at[part], sem, peer("core")).wait_recv()
-
-    def spread_x(part, o):
-        send(part, o, 0, "up")
-        send(part, o, 1, "down")
-        send(part, o, 1, "up")
-        send(part, o, 0, "down")
-
-    def first(part):
-        send(part, own, None, "z")
-        spread_x(part, own)
-        send(part, own, None, "core")
-
-    def second(part):
-        o = block(c, x, 1 - zl)
-        recv(part, o, None)
-        spread_x(part, o)
-        send(part, o, None, "core")
-
-    def third(part, zz):
-        lo, hi = block(c, x3, zz), block(c, x1, zz)
-        recv(part, lo, 0)
-        send(part, lo, 0, "up")
-        recv(part, hi, 1)
-        send(part, hi, 1, "down")
-        recv(part, lo, 1)
-        send(part, lo, None, "core")
-        recv(part, hi, 0)
-        send(part, hi, None, "core")
-
-    def fourth(part, zz):
-        o = block(c, x2, zz)
-        recv(part, o, 0)
-        recv(part, o, 1)
-        send(part, o, None, "core")
-
-    def fifth(part):
-        ref = bufs[part].at[pl.ds(8 * (1 - c), 8)]
-        remote(ref, ref, dsend.at[part], dcore.at[part], peer("core")).wait_recv()
-
     def zcopy(r, src):
         return remote(msg.at[pl.ds(2 * ((zh + r) % NZ), 2)], zm.at[src], zsend.at[r], zrecv.at[src], zdev(r))
 
@@ -170,7 +187,7 @@
         yput(src)
 
     def yput(src):
-        for r in range(1, NY):
+        for r in FAR:
             to = (y + r) % NY
             remote(zm.at[src, to // 4], xr.at[src, y], ysend.at[src], yrecv.at[src], ydev(r)).start()
         pltpu.make_async_copy(zm.at[src, y // 4], xr.at[src, y], yrecv.at[src]).start()
@@ -178,7 +195,6 @@
     for r in (1, 3, 2):
         zcopy(r, zh).start()
     zm[zh] = msg[pl.ds(2 * zh, 2)]
-    first(0)
     yput(zh)
 
     for cp in loads[4:7]:
@@ -199,6 +215,22 @@
             perm[pl.ds(base, 128), :] = jnp.where(
                 iota((128, D), 0) + base == omrow[...], 1.0, 0.0
             ).astype(BF)
+
+    def build_back(lo, hi):
+        @pl.loop(lo, hi)
+        def _(i):
+            here = jnp.broadcast_to(omrow[:, slots(i)].astype(F32), (128, 128)).T.astype(jnp.int32)
+            rows = pl.ds(pl.multiple_of(F + i * 128, 128), 128)
+            for u in range(16):
+                ptw[rows, 128 * u : 128 * u + 128] = jnp.where(
+                    iota((128, 128), 1) + 128 * u == here, 1.0, 0.0
+                ).astype(BF)
+
+    def turn():
+        @pl.loop(0, 8)
+        def _(i):
+            at = pl.ds(pl.multiple_of(i * 256, 256), 256)
+            ptw[:F, at] = w[at, 2 * F :].astype(F32).T.astype(BF)
 
     low = iota((64, 128), 1) < 64
 
@@ -219,37 +251,44 @@
         wacc = wacc + mm(xg[...], w[at, : 2 * F])
         lacc = lacc + mm(xg[...], router_ref[:, at], 1, 1)
 
-        @pl.loop(0, 4)
-        def _(i):
-            cols = pl.ds(pl.multiple_of(i * 512, 512), 512)
-            got = mm(xg[...], perm[at, cols])
-            if r == 0:
-                xacc[:, cols] = got
-            else:
-                xacc[:, cols] += got
-
+        got = mm(xg[...], perm[at, :])
+        if r == 0:
+            xacc[...] = got
+        elif r == 2:
+            xp[...] = (xacc[...] + got).astype(BF)
+        else:
+            xacc[...] += got
         return ssq, wacc, lacc
 
     build(0, 8)
+    pair(0)
+    onward(0, zl)
+    core(0, block(c, x, 1 - zl))
     zget(1)
     zget(3)
-    second(0)
+    pair(1)
+    onward(1, zl)
+    near(0, zl)
+    core(1, block(c, x, 1 - zl))
+    far(0, zl)
     zget(2)
-    first(1)
     build(8, 16)
-    third(0, zl)
-    second(1)
+    onward(0, 1 - zl)
     loads[7].wait()
+    turn()
     carry = (jnp.zeros((128, 128), F32), jnp.zeros((128, 2 * F), F32), jnp.zeros((128, NE), F32))
     carry = quarter(0, carry)
-    third(0, 1 - zl)
-    third(1, zl)
+    onward(1, 1 - zl)
+    near(1, zl)
+    near(0, 1 - zl)
+    build_back(0, 8)
+    far(1, zl)
     carry = quarter(1, carry)
-    fourth(0, zl)
-    fourth(0, 1 - zl)
-    third(1, 1 - zl)
+    far(0, 1 - zl)
     carry = quarter(3, carry)
-    fourth(1, zl)
+    near(1, 1 - zl)
+    build_back(8, 16)
+    far(1, 1 - zl)
     ssq, wacc, lacc = quarter(2, carry)
 
     scale = lax.rsqrt(jnp.sum(ssq, axis=-1, keepdims=True) * (1.0 / D) + 1e-06)
@@ -263,29 +302,28 @@
     this = jnp.sum(jnp.where(iota((128, NE), 1) == e0, sig, 0.0), axis=-1, keepdims=True)
     used = jnp.sum(chosen, axis=-1, keepdims=True) > 0.5
     share = jnp.where(used, this / jnp.where(used, total, 1.0), 0.0)
-    xp[...] = xacc[...].astype(BF)
 
     def halfmm(cc):
         at = pl.ds(pl.multiple_of(cc * (D // 2), D // 2), D // 2)
         return mm(xp[:, at], gu[pl.ds(8 * cc, 8)].reshape(D // 2, 2 * F))
 
     both = wacc + halfmm(c)
-    fifth(0)
+    other(0)
     both = (both + halfmm(1 - c)) * scale
     hidden = (jax.nn.silu(both[:, :F]) * both[:, F:] * share).astype(BF)
-    fourth(1, 1 - zl)
-    fifth(1)
-    xp[...] = mm(hidden, dn[...].reshape(D, F), 1, 1).astype(BF)
+    hy[:, :F] = hidden
+    other(1)
+    hy[:, F:] = mm(hidden, dn[...]).astype(BF)
 
     for r in (1, 2, 3, 0):
         zz = (zh + r) % NZ
         at = pl.ds(pl.multiple_of(zz * ZB, ZB), ZB)
-        part = mm(hidden, w[at, 2 * F :], 1, 1) + mm(xp[...], perm[at, :], 1, 1)
+        part = mm(hy[...], ptw[:, at])
         for u in range(NY // 2):
             even, odd = part[:64, 128 * u : 128 * u + 128], part[64:, 128 * u : 128 * u + 128]
             outm[zz, 2 * u] = jnp.where(low, even, pltpu.roll(odd, 64, 1)).astype(BF).reshape(2, CAP, 128)
             outm[zz, 2 * u + 1] = jnp.where(low, pltpu.roll(even, 64, 1), odd).astype(BF).reshape(2, CAP, 128)
-        for k in range(1, NY):
+        for k in FAR:
             remote(outm.at[zz, (y + k) % NY], outr.at[zz, y], osend.at[r], orecv.at[zz], ydev(k)).start()
         pltpu.make_async_copy(outm.at[zz, y], outr.at[zz, y], orecv.at[zz]).start()
 
@@ -317,7 +355,7 @@
         zcopy(r, zh).wait_send()
         pcopy(r, zh).wait_send()
     for part in range(2):
-        ref = bufs[part].at[pl.ds(0, 15)]
+        ref = gu.at[pl.ds(0, 15)] if part == 0 else dn.at[:, pl.ds(0, 15 * 128)]
         remote(ref, ref, dsend.at[part], dcore.at[part], peer("core")).wait_send()
     for r in range(NZ):
         ref = xr.at[r, pl.ds(0, NY - 1)]
@@ -345,8 +383,10 @@
             vm((1, D), jnp.int32),
             vm((D, 3 * F), BF),
             vm((16, 128, 2 * F), BF),
-            vm((16, 128, F), BF),
+            vm((F, D), BF),
             vm((D, D), BF),
+            vm((F + D, D), BF),
+            vm((128, F + D), BF),
             vm((256, 256), BF),
             vm((256, 256), BF),
             vm((NE, 2, CAP, 128), BF),

time: 57.2 us -> 52.7 us (0.921)
  Pallas kernels: 55.6 us -> 51 us
    pallas_call x1, Pallas kernels: 55.6 us -> 51 us  [body(): pl.pallas_call(kernel, out_shape=jax.ShapeDtypeStruct(tokens.shape, BF),...]
where the time goes in v4:
time: 52.7 us; the launch traced here: 52.5 us
  Pallas kernels  51 us (97%)
  local copies, waits for them, and re-layouts  1.47 us (3%)
    pallas_call x1, Pallas kernels, body(): pl.pallas_call(kernel, out_shape=jax.ShapeDtypeStruct(tokens.shape, BF),...  51 us
    unnamed x1, local copies, waits for them, and re-layouts  1.47 us

profile of v4, /device:TPU:1, one launch (start us, length us, event | category | flops | bytes accessed | tf_op | source)
XLA Modules:
  0.0 52.5 jit_solution(11273471330357652193)
XLA Ops:
  0.0 51.0 %shard_map.82 = bf16[4,64,64]{2,1,0:T(8,128)(2,1)} custom-call(bf16[4,64,64]{2,1,0:T(8,128)(2,1)} %tok_hbm.1, bf16[16,128]{1,0:T(8,128)(2,1)} %bitcast.8, bf16[8,2048]{1,0:T(8,128)(2,1)} %bitcast.5, s32[4,2,64]{2,1,0:T(2,128)} %bitcast.9, bf16[1,2048,768]{2,1,0:T(8,128)(2,1)} %w_hbm.1, bf16[1,128,768]{2,1,0:T(8,128)(2,1)} %codes_hbm.1, ...), custom_call_target="tpu_custom_call" | custom-call | flops 4000000000 | bytes 8388608 | tf_op jit(solution)/shard_map/pallas_call | solution.py:369
  51.0 1.5 %copy.10 = bf16[4,64,64]{2,1,0:T(8,128)(2,1)} copy(bf16[4,64,64]{2,1,0:T(8,128)(2,1)} %shard_map.82) | data formatting | bytes 65536

commit v5 on v4

--- a/solution.py
+++ b/solution.py
@@ -59,14 +59,16 @@
         (w_hbm.at[0], w),
     )
     loads = [pltpu.make_async_copy(a, b, wsem.at[i]) for i, (a, b) in enumerate(pairs)]
-    for cp in loads:
-        cp.start()
+    loads[0].start()
+    loads[1].start()
 
     bar = pltpu.get_barrier_semaphore()
     partners = [peer(k) for k in ("core", "z", "up", "down")]
     partners += [ydev(r) for r in range(1, NY)] + [zdev(r) for r in range(1, NZ)]
     for dev in partners:
         pl.semaphore_signal(bar, inc=1, device_id=dev, device_id_type=MESH)
+    for cp in loads[2:]:
+        cp.start()
 
     loads[0].wait()
     loads[1].wait()
@@ -102,16 +104,23 @@
     def core(part, o):
         send(part, o, None, "core")
 
+    def over(o):
+        remote(shard(1, o, None), shard(1, o, None), dsend.at[1], drecv.at[1, o, 0], peer("z")).start()
+
+    def both_ways(part):
+        send(part, own, 0, "up")
+        send(part, own, 1, "down")
+        send(part, own, 1, "up")
+        send(part, own, 0, "down")
+
     def first():
-        for part in range(2):
-            send(part, own, 0, "z")
-            send(part, own, 1, "z")
-            send(part, own, 0, "up")
-            send(part, own, 1, "down")
-            send(part, own, 1, "up")
-            send(part, own, 0, "down")
+        send(0, own, 0, "z")
+        send(0, own, 1, "z")
+        both_ways(1)
+        both_ways(0)
+        over(own)
+        core(1, own)
         core(0, own)
-        core(1, own)
 
     def pair(part):
         o = block(c, x, 1 - zl)
@@ -132,15 +141,30 @@
     def near(part, zz):
         lo, hi = block(c, x3, zz), block(c, x1, zz)
         recv(part, lo, 1)
-        core(part, lo)
+        if part == 1:
+            over(lo)
+        else:
+            core(part, lo)
         recv(part, hi, 0)
-        core(part, hi)
+        if part == 1:
+            over(hi)
+        else:
+            core(part, hi)
 
     def far(part, zz):
         o = block(c, x2, zz)
         recv(part, o, 0)
         recv(part, o, 1)
+        if part == 1:
+            over(o)
         core(part, o)
+
+    def across():
+        for xx in (x, x3, x1, x2):
+            o = block(c, xx, 1 - zl)
+            ref = shard(1, o, None)
+            remote(ref, ref, dsend.at[1], drecv.at[1, o, 0], peer("core")).wait_recv()
+            core(1, o)
 
     def other(part):
         ref = gu.at[pl.ds(8 * (1 - c), 8)] if part == 0 else dn.at[:, slots(8 * (1 - c), 8)]
@@ -260,43 +284,41 @@
             xacc[...] += got
         return ssq, wacc, lacc
 
-    build(0, 8)
-    pair(0)
-    onward(0, zl)
-    core(0, block(c, x, 1 - zl))
-    zget(1)
-    zget(3)
-    pair(1)
-    onward(1, zl)
-    near(0, zl)
-    core(1, block(c, x, 1 - zl))
-    far(0, zl)
-    zget(2)
-    build(8, 16)
-    onward(0, 1 - zl)
+    build(0, 16)
     loads[7].wait()
     turn()
-    carry = (jnp.zeros((128, 128), F32), jnp.zeros((128, 2 * F), F32), jnp.zeros((128, NE), F32))
-    carry = quarter(0, carry)
-    onward(1, 1 - zl)
-    near(1, zl)
-    near(0, 1 - zl)
-    build_back(0, 8)
-    far(1, zl)
-    carry = quarter(1, carry)
-    far(0, 1 - zl)
-    carry = quarter(3, carry)
-    near(1, 1 - zl)
-    build_back(8, 16)
-    far(1, 1 - zl)
-    ssq, wacc, lacc = quarter(2, carry)
-
-    scale = lax.rsqrt(jnp.sum(ssq, axis=-1, keepdims=True) * (1.0 / D) + 1e-06)
     mine = cmat[pl.ds(pl.multiple_of(e0 * CAP, CAP), CAP), :].astype(F32)
     four = jnp.concatenate([mine, mine, mine, mine], axis=0)
     rowid = iota((128, 256), 0)
     step = (rowid // 32 % 2) * 2 + rowid // 64
     chosen = mm(jnp.where(iota((128, 256), 1) // 64 == step, four, 0.0).astype(BF), hitb)[:, :NE]
+    build_back(0, 8)
+
+    onward(1, zl)
+    pair(0)
+    near(1, zl)
+    onward(0, zl)
+    build_back(8, 16)
+    core(1, block(c, x3, zl))
+    core(1, block(c, x1, zl))
+    core(0, block(c, x, 1 - zl))
+    zget(1)
+    zget(3)
+    far(1, zl)
+    near(0, zl)
+    zget(2)
+    onward(0, 1 - zl)
+    far(0, zl)
+    carry = (jnp.zeros((128, 128), F32), jnp.zeros((128, 2 * F), F32), jnp.zeros((128, NE), F32))
+    carry = quarter(0, carry)
+    across()
+    near(0, 1 - zl)
+    carry = quarter(1, carry)
+    far(0, 1 - zl)
+    carry = quarter(3, carry)
+    ssq, wacc, lacc = quarter(2, carry)
+
+    scale = lax.rsqrt(jnp.sum(ssq, axis=-1, keepdims=True) * (1.0 / D) + 1e-06)
     sig = jax.nn.sigmoid(lacc * scale) * chosen
     total = jnp.sum(sig, axis=-1, keepdims=True)
     this = jnp.sum(jnp.where(iota((128, NE), 1) == e0, sig, 0.0), axis=-1, keepdims=True)

time: 52.7 us -> 50.6 us (0.960)
  the two profiles are of different devices: /device:TPU:1 before, /device:TPU:8 now
where the time goes in v5:
time: 50.6 us; the launch traced here: 50.5 us
  Pallas kernels  49 us (97%)
  local copies, waits for them, and re-layouts  1.47 us (3%)
    pallas_call x1, Pallas kernels, body(): pl.pallas_call(kernel, out_shape=jax.ShapeDtypeStruct(tokens.shape, BF),...  49 us
    unnamed x1, local copies, waits for them, and re-layouts  1.47 us

profile of v5, /device:TPU:8, one launch (start us, length us, event | category | flops | bytes accessed | tf_op | source)
XLA Modules:
  0.0 50.5 jit_solution(1444431437824522260)
XLA Ops:
  0.0 49.0 %shard_map.82 = bf16[4,64,64]{2,1,0:T(8,128)(2,1)} custom-call(bf16[4,64,64]{2,1,0:T(8,128)(2,1)} %tok_hbm.1, bf16[16,128]{1,0:T(8,128)(2,1)} %bitcast.8, bf16[8,2048]{1,0:T(8,128)(2,1)} %bitcast.5, s32[4,2,64]{2,1,0:T(2,128)} %bitcast.9, bf16[1,2048,768]{2,1,0:T(8,128)(2,1)} %w_hbm.1, bf16[1,128,768]{2,1,0:T(8,128)(2,1)} %codes_hbm.1, ...), custom_call_target="tpu_custom_call" | custom-call | flops 4000000000 | bytes 8388608 | tf_op jit(solution)/shard_map/pallas_call | solution.py:391
  49.0 1.5 %copy.10 = bf16[4,64,64]{2,1,0:T(8,128)(2,1)} copy(bf16[4,64,64]{2,1,0:T(8,128)(2,1)} %shard_map.82) | data formatting | bytes 65536

commit v6 on v5

--- a/solution.py
+++ b/solution.py
@@ -25,7 +25,7 @@
 def kernel(
     tok_hbm, gain_hbm, router_hbm, routes_hbm, w_hbm, codes_hbm, scales_hbm, om_hbm, out_ref,
     tok_ref, gain_ref, router_ref, routes_ref, codes_ref, scales_ref, om_ref, grow, omrow,
-    w, gu, dn, perm, ptw, hy, cmat, ctmat, msg, zm, xr, xg, xacc, xp, outm, outr, zs, zr,
+    wd, gu, dn, wide, ptw, hy, cmat, ctmat, msg, zm, xr, xg, xacc, xp, outm, outr, zs, zr,
     wsem, dsend, drecv, dcore, zsend, zrecv, ysend, yrecv, osend, orecv, psend, precv,
 ):
     rep, tp, zl = lax.axis_index("rep"), lax.axis_index("tp"), lax.axis_index("fsdp")
@@ -56,15 +56,16 @@
     pairs = (
         (scales_hbm.at[0], scales_ref), (codes_hbm.at[0], codes_ref), (routes_hbm, routes_ref),
         (tok_hbm, tok_ref), (om_hbm, om_ref), (router_hbm, router_ref), (gain_hbm, gain_ref),
-        (w_hbm.at[0], w),
+        (w_hbm.at[0, :, pl.ds(0, 2 * F)], wide.at[:, pl.ds(D, 2 * F)]),
+        (w_hbm.at[0, :, pl.ds(2 * F, F)], wd),
     )
     loads = [pltpu.make_async_copy(a, b, wsem.at[i]) for i, (a, b) in enumerate(pairs)]
     loads[0].start()
     loads[1].start()
 
     bar = pltpu.get_barrier_semaphore()
-    partners = [peer(k) for k in ("core", "z", "up", "down")]
-    partners += [ydev(r) for r in range(1, NY)] + [zdev(r) for r in range(1, NZ)]
+    partners = [ydev(4), zdev(2), ydev(3), ydev(5), zdev(1), zdev(3)]
+    partners += [peer(k) for k in ("z", "up", "down", "core")] + [ydev(r) for r in (2, 6, 1, 7)]
     for dev in partners:
         pl.semaphore_signal(bar, inc=1, device_id=dev, device_id_type=MESH)
     for cp in loads[2:]:
@@ -236,7 +237,7 @@
         @pl.loop(lo, hi)
         def _(i):
             base = pl.multiple_of(i * 128, 128)
-            perm[pl.ds(base, 128), :] = jnp.where(
+            wide[pl.ds(base, 128), :D] = jnp.where(
                 iota((128, D), 0) + base == omrow[...], 1.0, 0.0
             ).astype(BF)
 
@@ -254,14 +255,13 @@
         @pl.loop(0, 8)
         def _(i):
             at = pl.ds(pl.multiple_of(i * 256, 256), 256)
-            ptw[:F, at] = w[at, 2 * F :].astype(F32).T.astype(BF)
+            ptw[:F, at] = wd[at, :].astype(F32).T.astype(BF)
 
     low = iota((64, 128), 1) < 64
 
-    def quarter(r, carry):
+    def quarter(r, ssq):
         zz = (zh + r) % NZ
         remote(xr.at[zz], xr.at[zz], ysend.at[zz], yrecv.at[zz], ydev(1)).wait_recv()
-        ssq, wacc, lacc = carry
         for u in range(NY // 2):
             a = xr[zz, 2 * u].reshape(64, 128).astype(F32)
             b = xr[zz, 2 * u + 1].reshape(64, 128).astype(F32)
@@ -272,21 +272,21 @@
             xg[:64, 128 * u : 128 * u + 128] = (even * g).astype(BF)
             xg[64:, 128 * u : 128 * u + 128] = (odd * g).astype(BF)
         at = pl.ds(pl.multiple_of(zz * ZB, ZB), ZB)
-        wacc = wacc + mm(xg[...], w[at, : 2 * F])
-        lacc = lacc + mm(xg[...], router_ref[:, at], 1, 1)
-
-        got = mm(xg[...], perm[at, :])
+        got = mm(xg[...], wide[at, :])
         if r == 0:
             xacc[...] = got
-        elif r == 2:
-            xp[...] = (xacc[...] + got).astype(BF)
         else:
             xacc[...] += got
-        return ssq, wacc, lacc
+        return ssq
 
     build(0, 16)
     loads[7].wait()
+    loads[8].wait()
     turn()
+    for u in range(16):
+        names = router_ref[:, 128 * u : 128 * u + 128].astype(F32)
+        tall = jnp.concatenate([names, jnp.zeros((128 - NE, 128), F32)], axis=0)
+        wide[128 * u : 128 * u + 128, D + 2 * F :] = tall.T.astype(BF)
     mine = cmat[pl.ds(pl.multiple_of(e0 * CAP, CAP), CAP), :].astype(F32)
     four = jnp.concatenate([mine, mine, mine, mine], axis=0)
     rowid = iota((128, 256), 0)
@@ -309,17 +309,17 @@
     zget(2)
     onward(0, 1 - zl)
     far(0, zl)
-    carry = (jnp.zeros((128, 128), F32), jnp.zeros((128, 2 * F), F32), jnp.zeros((128, NE), F32))
-    carry = quarter(0, carry)
+    ssq = quarter(0, jnp.zeros((128, 128), F32))
     across()
     near(0, 1 - zl)
-    carry = quarter(1, carry)
+    ssq = quarter(1, ssq)
     far(0, 1 - zl)
-    carry = quarter(3, carry)
-    ssq, wacc, lacc = quarter(2, carry)
+    ssq = quarter(3, ssq)
+    ssq = quarter(2, ssq)
+    xp[...] = xacc[:, :D].astype(BF)
 
     scale = lax.rsqrt(jnp.sum(ssq, axis=-1, keepdims=True) * (1.0 / D) + 1e-06)
-    sig = jax.nn.sigmoid(lacc * scale) * chosen
+    sig = jax.nn.sigmoid(xacc[:, D + 2 * F : D + 2 * F + NE] * scale) * chosen
     total = jnp.sum(sig, axis=-1, keepdims=True)
     this = jnp.sum(jnp.where(iota((128, NE), 1) == e0, sig, 0.0), axis=-1, keepdims=True)
     used = jnp.sum(chosen, axis=-1, keepdims=True) > 0.5
@@ -329,7 +329,7 @@
         at = pl.ds(pl.multiple_of(cc * (D // 2), D // 2), D // 2)
         return mm(xp[:, at], gu[pl.ds(8 * cc, 8)].reshape(D // 2, 2 * F))
 
-    both = wacc + halfmm(c)
+    both = xacc[:, D : D + 2 * F] + halfmm(c)
     other(0)
     both = (both + halfmm(1 - c)) * scale
     hidden = (jax.nn.silu(both[:, :F]) * both[:, F:] * share).astype(BF)
@@ -337,16 +337,23 @@
     other(1)
     hy[:, F:] = mm(hidden, dn[...]).astype(BF)
 
+    near_y, far_y = 4 * (y // 4), 4 * (1 - y // 4)
+    dests = (
+        [far_y + (y + k) % 4 for k in (0, 1, 3, 2)],
+        [near_y + (y + k) % 4 for k in (2, 1, 3)],
+    )
     for r in (1, 2, 3, 0):
         zz = (zh + r) % NZ
-        at = pl.ds(pl.multiple_of(zz * ZB, ZB), ZB)
-        part = mm(hy[...], ptw[:, at])
-        for u in range(NY // 2):
-            even, odd = part[:64, 128 * u : 128 * u + 128], part[64:, 128 * u : 128 * u + 128]
-            outm[zz, 2 * u] = jnp.where(low, even, pltpu.roll(odd, 64, 1)).astype(BF).reshape(2, CAP, 128)
-            outm[zz, 2 * u + 1] = jnp.where(low, pltpu.roll(even, 64, 1), odd).astype(BF).reshape(2, CAP, 128)
-        for k in FAR:
-            remote(outm.at[zz, (y + k) % NY], outr.at[zz, y], osend.at[r], orecv.at[zz], ydev(k)).start()
+        for i, hb in enumerate((1 - y // 4, y // 4)):
+            part = mm(hy[...], ptw[:, pl.ds(pl.multiple_of(zz * ZB + hb * 256, 256), 256)])
+            for u in range(2):
+                even, odd = part[:64, 128 * u : 128 * u + 128], part[64:, 128 * u : 128 * u + 128]
+                outm[zz, 4 * hb + 2 * u] = jnp.where(low, even, pltpu.roll(odd, 64, 1)).astype(BF).reshape(2, CAP, 128)
+                outm[zz, 4 * hb + 2 * u + 1] = jnp.where(low, pltpu.roll(even, 64, 1), odd).astype(BF).reshape(2, CAP, 128)
+            for to in dests[i]:
+                remote(
+                    outm.at[zz, to], outr.at[zz, y], osend.at[r], orecv.at[zz], {"tp": zh * NY + to}
+                ).start()
         pltpu.make_async_copy(outm.at[zz, y], outr.at[zz, y], orecv.at[zz]).start()
 
     def sums(r):
@@ -403,10 +410,10 @@
             vm((1, D), jnp.int32),
             vm((1, D), F32),
             vm((1, D), jnp.int32),
-            vm((D, 3 * F), BF),
+            vm((D, F), BF),
             vm((16, 128, 2 * F), BF),
             vm((F, D), BF),
-            vm((D, D), BF),
+            vm((D, D + 2 * F + 128), BF),
             vm((F + D, D), BF),
             vm((128, F + D), BF),
             vm((256, 256), BF),
@@ -415,13 +422,13 @@
             vm((NZ, 2, 2, CAP, 128), BF),
             vm((NZ, NY, 2, CAP, 128), BF),
             vm((128, ZB), BF),
-            vm((128, D), F32),
+            vm((128, D + 2 * F + 128), F32),
             vm((128, D), BF),
             vm((NZ, NY, 2, CAP, 128), BF),
             vm((NZ, NY, 2, CAP, 128), BF),
             vm((NZ, 2, 2, CAP, 128), BF),
             vm((NZ, 2, 2, CAP, 128), BF),
-            dma((8,)), dma((2,)), dma((2, 16, 2)), dma((2,)),
+            dma((9,)), dma((2,)), dma((2, 16, 2)), dma((2,)),
             dma((NZ,)), dma((NZ,)), dma((NZ,)), dma((NZ,)),
             dma((NZ,)), dma((NZ,)), dma((NZ,)), dma((NZ,)),
         ],

time: 50.6 us -> 50.3 us (level)
  no operation moved by 1% of the time
where the time goes in v6:
time: 50.3 us; the launch traced here: 50.2 us
  Pallas kernels  48.7 us (97%)
  local copies, waits for them, and re-layouts  1.47 us (3%)
    pallas_call x1, Pallas kernels, body(): pl.pallas_call(kernel, out_shape=jax.ShapeDtypeStruct(tokens.shape, BF),...  48.7 us
    unnamed x1, local copies, waits for them, and re-layouts  1.47 us

profile of v6, /device:TPU:8, one launch (start us, length us, event | category | flops | bytes accessed | tf_op | source)
XLA Modules:
  0.0 50.2 jit_solution(18244877812235575441)
XLA Ops:
  0.0 48.7 %shard_map.82 = bf16[4,64,64]{2,1,0:T(8,128)(2,1)} custom-call(bf16[4,64,64]{2,1,0:T(8,128)(2,1)} %tok_hbm.1, bf16[16,128]{1,0:T(8,128)(2,1)} %bitcast.8, bf16[8,2048]{1,0:T(8,128)(2,1)} %bitcast.5, s32[4,2,64]{2,1,0:T(2,128)} %bitcast.9, bf16[1,2048,768]{2,1,0:T(8,128)(2,1)} %w_hbm.1, bf16[1,128,768]{2,1,0:T(8,128)(2,1)} %codes_hbm.1, ...), custom_call_target="tpu_custom_call" | custom-call | flops 4000000000 | bytes 8388608 | tf_op jit(solution)/shard_map/pallas_call | solution.py:398
  48.7 1.5 %copy.10 = bf16[4,64,64]{2,1,0:T(8,128)(2,1)} copy(bf16[4,64,64]{2,1,0:T(8,128)(2,1)} %shard_map.82) | data formatting | bytes 65536

commit v7 on v6

--- a/solution.py
+++ b/solution.py
@@ -68,8 +68,8 @@
     partners += [peer(k) for k in ("z", "up", "down", "core")] + [ydev(r) for r in (2, 6, 1, 7)]
     for dev in partners:
         pl.semaphore_signal(bar, inc=1, device_id=dev, device_id_type=MESH)
-    for cp in loads[2:]:
-        cp.start()
+    loads[2].start()
+    loads[3].start()
 
     loads[0].wait()
     loads[1].wait()
@@ -172,6 +172,8 @@
         remote(ref, ref, dsend.at[part], dcore.at[part], peer("core")).wait_recv()
 
     first()
+    for cp in loads[4:]:
+        cp.start()
 
     loads[2].wait()
     loads[3].wait()

time: 50.3 us -> 50.4 us (level)
  no operation moved by 1% of the time
where the time goes in v7:
time: 50.4 us; the launch traced here: 50.2 us
  Pallas kernels  48.7 us (97%)
  local copies, waits for them, and re-layouts  1.47 us (3%)
    pallas_call x1, Pallas kernels, body(): pl.pallas_call(kernel, out_shape=jax.ShapeDtypeStruct(tokens.shape, BF),...  48.7 us
    unnamed x1, local copies, waits for them, and re-layouts  1.47 us

profile of v7, /device:TPU:8, one launch (start us, length us, event | category | flops | bytes accessed | tf_op | source)
XLA Modules:
  0.0 50.2 jit_solution(3330475109430799971)
XLA Ops:
  0.0 48.7 %shard_map.82 = bf16[4,64,64]{2,1,0:T(8,128)(2,1)} custom-call(bf16[4,64,64]{2,1,0:T(8,128)(2,1)} %tok_hbm.1, bf16[16,128]{1,0:T(8,128)(2,1)} %bitcast.8, bf16[8,2048]{1,0:T(8,128)(2,1)} %bitcast.5, s32[4,2,64]{2,1,0:T(2,128)} %bitcast.9, bf16[1,2048,768]{2,1,0:T(8,128)(2,1)} %w_hbm.1, bf16[1,128,768]{2,1,0:T(8,128)(2,1)} %codes_hbm.1, ...), custom_call_target="tpu_custom_call" | custom-call | flops 4000000000 | bytes 8388608 | tf_op jit(solution)/shard_map/pallas_call | solution.py:400
  48.7 1.5 %copy.10 = bf16[4,64,64]{2,1,0:T(8,128)(2,1)} copy(bf16[4,64,64]{2,1,0:T(8,128)(2,1)} %shard_map.82) | data formatting | bytes 65536

commit v8 on v7

--- a/solution.py
+++ b/solution.py
@@ -64,8 +64,9 @@
     loads[1].start()
 
     bar = pltpu.get_barrier_semaphore()
-    partners = [ydev(4), zdev(2), ydev(3), ydev(5), zdev(1), zdev(3)]
-    partners += [peer(k) for k in ("z", "up", "down", "core")] + [ydev(r) for r in (2, 6, 1, 7)]
+    partners = [peer(k) for k in ("z", "up", "down", "core")]
+    partners += [ydev(4), zdev(2), ydev(3), ydev(5), zdev(1), zdev(3)]
+    partners += [ydev(r) for r in (2, 6, 1, 7)]
     for dev in partners:
         pl.semaphore_signal(bar, inc=1, device_id=dev, device_id_type=MESH)
     loads[2].start()

time: 50.4 us -> 51.1 us (1.014)
  Pallas kernels: 48.7 us -> 49.4 us
    pallas_call x1, Pallas kernels: 48.7 us -> 49.4 us  [body(): pl.pallas_call(kernel, out_shape=jax.ShapeDtypeStruct(tokens.shape, BF),...]
where the time goes in v8:
time: 51.1 us; the launch traced here: 50.9 us
  Pallas kernels  49.4 us (97%)
  local copies, waits for them, and re-layouts  1.47 us (3%)
    pallas_call x1, Pallas kernels, body(): pl.pallas_call(kernel, out_shape=jax.ShapeDtypeStruct(tokens.shape, BF),...  49.4 us
    unnamed x1, local copies, waits for them, and re-layouts  1.47 us

profile of v8, /device:TPU:8, one launch (start us, length us, event | category | flops | bytes accessed | tf_op | source)
XLA Modules:
  0.0 50.9 jit_solution(15711455233542421760)
XLA Ops:
  0.0 49.4 %shard_map.82 = bf16[4,64,64]{2,1,0:T(8,128)(2,1)} custom-call(bf16[4,64,64]{2,1,0:T(8,128)(2,1)} %tok_hbm.1, bf16[16,128]{1,0:T(8,128)(2,1)} %bitcast.8, bf16[8,2048]{1,0:T(8,128)(2,1)} %bitcast.5, s32[4,2,64]{2,1,0:T(2,128)} %bitcast.9, bf16[1,2048,768]{2,1,0:T(8,128)(2,1)} %w_hbm.1, bf16[1,128,768]{2,1,0:T(8,128)(2,1)} %codes_hbm.1, ...), custom_call_target="tpu_custom_call" | custom-call | flops 4000000000 | bytes 8388608 | tf_op jit(solution)/shard_map/pallas_call | solution.py:401
  49.4 1.5 %copy.10 = bf16[4,64,64]{2,1,0:T(8,128)(2,1)} copy(bf16[4,64,64]{2,1,0:T(8,128)(2,1)} %shard_map.82) | data formatting | bytes 65536
